TPU v7x, 1024 devices: a whole 4x4x32 slice. The times are simulated.
1024 devices in a mesh: sect: 8 (over y, core), blk: 32 (over x, z_lo), obs: 4 (over z_hi).
Axes of the slice: x: 4, y: 4, z: 32 (z_hi: 4, z_lo: 8; z = z_hi * 8 + z_lo), core: 2. Of those that a mesh axis runs over, the one named last changes fastest.
Arguments:
- series: float32 [2, 16384, 512], P(None, ('sect', 'blk'), 'obs'), may hold values from -6 to 6
- positions: float32 [3, 16384], P(None, ('sect', 'blk')), may hold values from -1 to 1
- normals: float32 [3, 16384], P(None, ('sect', 'blk')), may hold values from -1 to 1
- areas: float32 [16384], P(('sect', 'blk')), may hold values from 0.3 to 3
- counts: int32 [256], P(('sect', 'blk')), may hold values from 1 to 64, 8192 in all
- observers: float32 [3, 4096], P(None, 'blk'), may hold values from -8 to 8, as said below
Outputs:
- pressure: float32 [2, 64, 4096], P(None, 'obs', 'blk')
Inputs may be any that keep to these rules, and one draw needn't show every extreme that they name: The counts over all 256 tiles sum to 8192 and the largest is 64. `observers`: every observer lies between 2 and 8 from the anchor.
All inputs are finite; a program needn't handle non-finite values. No bound on the sum of `counts` on one device may be relied on, other than what follows from the above.
Results may differ from a plain program's by a relative error of at most 0.0003.
Values sent between devices are 32-bit elements; how exact they have to be, the bound alone decides.
No kernel may reach another device: no remote copies, remote signals or barrier semaphores. Data moves between devices by JAX's collectives and lax.ppermute only.
A program may use at most 32 MiB of HBM per device.

v0:
```python
import math

import jax
import jax.numpy as jnp
from jax import lax
from jax.sharding import PartitionSpec as P

SAMPLES = 512
FREQS = 64


WAVE_SCALE = 0.05
FOUR_PI = 4.0 * math.pi


def spectrum(series, frequency_indices, time_steps):
    products = frequency_indices[:, None] * time_steps[None, :] % SAMPLES
    angles = 2.0 * math.pi / SAMPLES * products.astype(jnp.float32)
    dft_scale = SAMPLES ** (-0.5)
    cosines = jnp.cos(angles) * dft_scale
    sines = -jnp.sin(angles) * dft_scale
    real_part = jnp.einsum("ft,cpt->fcp", cosines, series, precision=lax.Precision.HIGHEST)
    imag_part = jnp.einsum("ft,cpt->fcp", sines, series, precision=lax.Precision.HIGHEST)
    return jnp.concatenate([real_part, imag_part], axis=1)


def panel_field(observers, geometry, spectra, wave_numbers):
    offset = observers[:, :, None] - geometry[0][:, None, :]
    radial_separation = jnp.sqrt(jnp.sum(offset * offset, axis=0))
    cosine = jnp.sum(geometry[1][:, None, :] * offset, axis=0) / radial_separation
    spherical_decay = 1.0 / (FOUR_PI * radial_separation)

    def single(element):
        wavenum, emitter_panel = element
        thick_real, load_real, thick_imag, load_imag = (
            emitter_panel[0],
            emitter_panel[1],
            emitter_panel[2],
            emitter_panel[3],
        )
        phases = wavenum * radial_separation
        cos_phase = jnp.cos(phases)
        sin_phase = jnp.sin(phases)
        amp_real = -wavenum * thick_imag + cosine * (
            load_real / radial_separation - wavenum * load_imag
        )
        amp_imag = wavenum * thick_real + cosine * (
            load_imag / radial_separation + wavenum * load_real
        )
        out_real = jnp.sum(spherical_decay * (cos_phase * amp_real + sin_phase * amp_imag), axis=1)
        out_imag = jnp.sum(spherical_decay * (cos_phase * amp_imag - sin_phase * amp_real), axis=1)
        return jnp.stack([out_real, out_imag])

    return lax.map(single, (wave_numbers, jnp.swapaxes(spectra, 0, 1)))


def body(series, positions, normals, areas, counts, observers):
    group_count = lax.axis_size("obs")
    per_group = FREQS // group_count
    group_index = lax.axis_index("obs")
    slot_count = series.shape[1]
    time_local = series.shape[2]
    is_live = jnp.arange(slot_count, dtype=jnp.int32) < counts[0]
    weights = areas * is_live.astype(jnp.float32)
    time_steps = group_index * time_local + jnp.arange(time_local, dtype=jnp.int32)
    frequency_indices = (
        jnp.int32(0) + 1 + jnp.arange(lax.axis_size("obs") * per_group, dtype=jnp.int32)
    )
    spectra = lax.psum_scatter(
        spectrum(series, frequency_indices, time_steps).reshape(
            lax.axis_size("obs") * per_group, 4 * slot_count
        ),
        "obs",
        scatter_dimension=0,
        tiled=True,
    ).reshape(per_group, 4, slot_count)
    sources = jnp.swapaxes(spectra, 0, 1) * weights
    geometry = jnp.stack([positions, normals])
    wave_numbers = WAVE_SCALE * (
        group_index * per_group + 1 + jnp.arange(per_group, dtype=jnp.int32)
    ).astype(jnp.float32)
    pressure_part = panel_field(
        observers,
        lax.all_gather(geometry, "blk", axis=2, tiled=True),
        lax.all_gather(sources, "blk", axis=2, tiled=True),
        wave_numbers,
    )
    combined = lax.psum(pressure_part, "sect")
    return jnp.swapaxes(combined, 0, 1)


def solution(mesh):
    placed = (
        P(None, ("sect", "blk"), "obs"),
        P(None, ("sect", "blk")),
        P(None, ("sect", "blk")),
        P(("sect", "blk")),
        P(("sect", "blk")),
        P(None, "blk"),
    )
    return jax.shard_map(
        body, mesh=mesh, in_specs=placed, out_specs=P(None, "obs", "blk"), check_vma=False
    )
```

profile of v0, /device:TPU:1, one launch (start us, length us, event | category | flops | bytes accessed | tf_op | source)
XLA Modules:
  0.0 511.4 jit_solution(10749805882966774615)
XLA Ops:
  10.6 133.1 %all_gather.6 = f32[2,3,2048]{1,0,2:T(2,128)S(1)} all-gather(f32[2,3,64]{1,0,2:T(2,128)S(1)} %copy.39), channel_id=1, replica_groups=mesh['sect'=8,'blk'=32,'obs'=4] {'blk'}, dimensions={2}, use_global_device_ids=true | all-gather | bytes 50688 | tf_op jit(solution)/shard_map/all_gather | solution.py:84
  143.7 2.4 fusion.29
  151.2 155.7 %all_gather.7 = f32[4,16,2048]{1,0,2:T(4,128)} all-gather(f32[4,16,64]{1,0,2:T(4,128)S(1)} %copy.43), channel_id=1, replica_groups=mesh['sect'=8,'blk'=32,'obs'=4] {'blk'}, dimensions={2}, use_global_device_ids=true | all-gather | bytes 540672 | tf_op jit(solution)/shard_map/all_gather | solution.py:85
  306.9 4.5 copy.45
  311.5 151.5 %while.10 = (s32[]{:T(128)}, f32[16,2,128]{2,0,1:T(8,128)S(1)}, f32[16]{0:T(128)S(1)}, f32[128,2048]{1,0:T(8,128)S(1)}, f32[16,4,2048]{2,1,0:T(4,128)}, /*index=...) while((s32[]{:T(128)}, f32[16,2,128]{2,0,1:T(8,128)S(1)}, ...), condition=%wide.region_6.7_spmd, body=%wide.region_3.6_spmd.sunk | while | flops 4988934 | bytes 3298513 | solution.py:54
  312.8 1.6 dynamic-slice_multiply_fusion.3
  315.1 5.7 %multiply_reduce_fusion.3 = (f32[128]{0:T(128)S(1)}, f32[128]{0:T(128)S(1)}) fusion(f32[128,2048]{1,0:T(8,128)S(1)} %get-tuple-element.196, f32[128,2048]{1,0:T(8,128)S(1)} %get-tuple-element.193, f32[128,2048]{1,0:T(8,128)S(1)} %get-tuple-element.195, f32[2048]{0:T(1024)S(1)} %get-tuple-element.160, f32[2048]{0:T(1024)S(1)} %bitcast.46, ...), kind=kLoop, calls=%fused_computation.1.clone.1 | loop fusion | flops 4980480 | bytes 3195908 | tf_op jit(solution)/shard_map/while/body/eval_jaxpr/reduce_sum | solution.py:50
  322.3 1.7 dynamic-slice_multiply_fusion.3
  324.6 5.7 %multiply_reduce_fusion.3 = (f32[128]{0:T(128)S(1)}, f32[128]{0:T(128)S(1)}) fusion(f32[128,2048]{1,0:T(8,128)S(1)} %get-tuple-element.196, f32[128,2048]{1,0:T(8,128)S(1)} %get-tuple-element.193, f32[128,2048]{1,0:T(8,128)S(1)} %get-tuple-element.195, f32[2048]{0:T(1024)S(1)} %get-tuple-element.160, f32[2048]{0:T(1024)S(1)} %bitcast.46, ...), kind=kLoop, calls=%fused_computation.1.clone.1 | loop fusion | flops 4980480 | bytes 3195908 | tf_op jit(solution)/shard_map/while/body/eval_jaxpr/reduce_sum | solution.py:50
  331.8 1.6 dynamic-slice_multiply_fusion.3
  334.1 5.7 %multiply_reduce_fusion.3 = (f32[128]{0:T(128)S(1)}, f32[128]{0:T(128)S(1)}) fusion(f32[128,2048]{1,0:T(8,128)S(1)} %get-tuple-element.196, f32[128,2048]{1,0:T(8,128)S(1)} %get-tuple-element.193, f32[128,2048]{1,0:T(8,128)S(1)} %get-tuple-element.195, f32[2048]{0:T(1024)S(1)} %get-tuple-element.160, f32[2048]{0:T(1024)S(1)} %bitcast.46, ...), kind=kLoop, calls=%fused_computation.1.clone.1 | loop fusion | flops 4980480 | bytes 3195908 | tf_op jit(solution)/shard_map/while/body/eval_jaxpr/reduce_sum | solution.py:50
  341.2 1.6 dynamic-slice_multiply_fusion.3
  343.6 5.7 %multiply_reduce_fusion.3 = (f32[128]{0:T(128)S(1)}, f32[128]{0:T(128)S(1)}) fusion(f32[128,2048]{1,0:T(8,128)S(1)} %get-tuple-element.196, f32[128,2048]{1,0:T(8,128)S(1)} %get-tuple-element.193, f32[128,2048]{1,0:T(8,128)S(1)} %get-tuple-element.195, f32[2048]{0:T(1024)S(1)} %get-tuple-element.160, f32[2048]{0:T(1024)S(1)} %bitcast.46, ...), kind=kLoop, calls=%fused_computation.1.clone.1 | loop fusion | flops 4980480 | bytes 3195908 | tf_op jit(solution)/shard_map/while/body/eval_jaxpr/reduce_sum | solution.py:50
  350.7 1.6 dynamic-slice_multiply_fusion.3
  353.0 5.7 %multiply_reduce_fusion.3 = (f32[128]{0:T(128)S(1)}, f32[128]{0:T(128)S(1)}) fusion(f32[128,2048]{1,0:T(8,128)S(1)} %get-tuple-element.196, f32[128,2048]{1,0:T(8,128)S(1)} %get-tuple-element.193, f32[128,2048]{1,0:T(8,128)S(1)} %get-tuple-element.195, f32[2048]{0:T(1024)S(1)} %get-tuple-element.160, f32[2048]{0:T(1024)S(1)} %bitcast.46, ...), kind=kLoop, calls=%fused_computation.1.clone.1 | loop fusion | flops 4980480 | bytes 3195908 | tf_op jit(solution)/shard_map/while/body/eval_jaxpr/reduce_sum | solution.py:50
  360.2 1.6 dynamic-slice_multiply_fusion.3
  362.5 5.7 %multiply_reduce_fusion.3 = (f32[128]{0:T(128)S(1)}, f32[128]{0:T(128)S(1)}) fusion(f32[128,2048]{1,0:T(8,128)S(1)} %get-tuple-element.196, f32[128,2048]{1,0:T(8,128)S(1)} %get-tuple-element.193, f32[128,2048]{1,0:T(8,128)S(1)} %get-tuple-element.195, f32[2048]{0:T(1024)S(1)} %get-tuple-element.160, f32[2048]{0:T(1024)S(1)} %bitcast.46, ...), kind=kLoop, calls=%fused_computation.1.clone.1 | loop fusion | flops 4980480 | bytes 3195908 | tf_op jit(solution)/shard_map/while/body/eval_jaxpr/reduce_sum | solution.py:50
  369.6 1.6 dynamic-slice_multiply_fusion.3
  372.0 5.7 %multiply_reduce_fusion.3 = (f32[128]{0:T(128)S(1)}, f32[128]{0:T(128)S(1)}) fusion(f32[128,2048]{1,0:T(8,128)S(1)} %get-tuple-element.196, f32[128,2048]{1,0:T(8,128)S(1)} %get-tuple-element.193, f32[128,2048]{1,0:T(8,128)S(1)} %get-tuple-element.195, f32[2048]{0:T(1024)S(1)} %get-tuple-element.160, f32[2048]{0:T(1024)S(1)} %bitcast.46, ...), kind=kLoop, calls=%fused_computation.1.clone.1 | loop fusion | flops 4980480 | bytes 3195908 | tf_op jit(solution)/shard_map/while/body/eval_jaxpr/reduce_sum | solution.py:50
  381.4 5.7 %multiply_reduce_fusion.3 = (f32[128]{0:T(128)S(1)}, f32[128]{0:T(128)S(1)}) fusion(f32[128,2048]{1,0:T(8,128)S(1)} %get-tuple-element.196, f32[128,2048]{1,0:T(8,128)S(1)} %get-tuple-element.193, f32[128,2048]{1,0:T(8,128)S(1)} %get-tuple-element.195, f32[2048]{0:T(1024)S(1)} %get-tuple-element.160, f32[2048]{0:T(1024)S(1)} %bitcast.46, ...), kind=kLoop, calls=%fused_computation.1.clone.1 | loop fusion | flops 4980480 | bytes 3195908 | tf_op jit(solution)/shard_map/while/body/eval_jaxpr/reduce_sum | solution.py:50
  388.6 1.6 dynamic-slice_multiply_fusion.3
  390.9 5.7 %multiply_reduce_fusion.3 = (f32[128]{0:T(128)S(1)}, f32[128]{0:T(128)S(1)}) fusion(f32[128,2048]{1,0:T(8,128)S(1)} %get-tuple-element.196, f32[128,2048]{1,0:T(8,128)S(1)} %get-tuple-element.193, f32[128,2048]{1,0:T(8,128)S(1)} %get-tuple-element.195, f32[2048]{0:T(1024)S(1)} %get-tuple-element.160, f32[2048]{0:T(1024)S(1)} %bitcast.46, ...), kind=kLoop, calls=%fused_computation.1.clone.1 | loop fusion | flops 4980480 | bytes 3195908 | tf_op jit(solution)/shard_map/while/body/eval_jaxpr/reduce_sum | solution.py:50
  398.0 1.6 dynamic-slice_multiply_fusion.3
  400.4 5.7 %multiply_reduce_fusion.3 = (f32[128]{0:T(128)S(1)}, f32[128]{0:T(128)S(1)}) fusion(f32[128,2048]{1,0:T(8,128)S(1)} %get-tuple-element.196, f32[128,2048]{1,0:T(8,128)S(1)} %get-tuple-element.193, f32[128,2048]{1,0:T(8,128)S(1)} %get-tuple-element.195, f32[2048]{0:T(1024)S(1)} %get-tuple-element.160, f32[2048]{0:T(1024)S(1)} %bitcast.46, ...), kind=kLoop, calls=%fused_computation.1.clone.1 | loop fusion | flops 4980480 | bytes 3195908 | tf_op jit(solution)/shard_map/while/body/eval_jaxpr/reduce_sum | solution.py:50
  407.5 1.6 dynamic-slice_multiply_fusion.3
  409.8 5.7 %multiply_reduce_fusion.3 = (f32[128]{0:T(128)S(1)}, f32[128]{0:T(128)S(1)}) fusion(f32[128,2048]{1,0:T(8,128)S(1)} %get-tuple-element.196, f32[128,2048]{1,0:T(8,128)S(1)} %get-tuple-element.193, f32[128,2048]{1,0:T(8,128)S(1)} %get-tuple-element.195, f32[2048]{0:T(1024)S(1)} %get-tuple-element.160, f32[2048]{0:T(1024)S(1)} %bitcast.46, ...), kind=kLoop, calls=%fused_computation.1.clone.1 | loop fusion | flops 4980480 | bytes 3195908 | tf_op jit(solution)/shard_map/while/body/eval_jaxpr/reduce_sum | solution.py:50
  419.3 5.7 %multiply_reduce_fusion.3 = (f32[128]{0:T(128)S(1)}, f32[128]{0:T(128)S(1)}) fusion(f32[128,2048]{1,0:T(8,128)S(1)} %get-tuple-element.196, f32[128,2048]{1,0:T(8,128)S(1)} %get-tuple-element.193, f32[128,2048]{1,0:T(8,128)S(1)} %get-tuple-element.195, f32[2048]{0:T(1024)S(1)} %get-tuple-element.160, f32[2048]{0:T(1024)S(1)} %bitcast.46, ...), kind=kLoop, calls=%fused_computation.1.clone.1 | loop fusion | flops 4980480 | bytes 3195908 | tf_op jit(solution)/shard_map/while/body/eval_jaxpr/reduce_sum | solution.py:50
  428.8 5.7 %multiply_reduce_fusion.3 = (f32[128]{0:T(128)S(1)}, f32[128]{0:T(128)S(1)}) fusion(f32[128,2048]{1,0:T(8,128)S(1)} %get-tuple-element.196, f32[128,2048]{1,0:T(8,128)S(1)} %get-tuple-element.193, f32[128,2048]{1,0:T(8,128)S(1)} %get-tuple-element.195, f32[2048]{0:T(1024)S(1)} %get-tuple-element.160, f32[2048]{0:T(1024)S(1)} %bitcast.46, ...), kind=kLoop, calls=%fused_computation.1.clone.1 | loop fusion | flops 4980480 | bytes 3195908 | tf_op jit(solution)/shard_map/while/body/eval_jaxpr/reduce_sum | solution.py:50
  438.2 5.7 %multiply_reduce_fusion.3 = (f32[128]{0:T(128)S(1)}, f32[128]{0:T(128)S(1)}) fusion(f32[128,2048]{1,0:T(8,128)S(1)} %get-tuple-element.196, f32[128,2048]{1,0:T(8,128)S(1)} %get-tuple-element.193, f32[128,2048]{1,0:T(8,128)S(1)} %get-tuple-element.195, f32[2048]{0:T(1024)S(1)} %get-tuple-element.160, f32[2048]{0:T(1024)S(1)} %bitcast.46, ...), kind=kLoop, calls=%fused_computation.1.clone.1 | loop fusion | flops 4980480 | bytes 3195908 | tf_op jit(solution)/shard_map/while/body/eval_jaxpr/reduce_sum | solution.py:50
  447.7 5.7 %multiply_reduce_fusion.3 = (f32[128]{0:T(128)S(1)}, f32[128]{0:T(128)S(1)}) fusion(f32[128,2048]{1,0:T(8,128)S(1)} %get-tuple-element.196, f32[128,2048]{1,0:T(8,128)S(1)} %get-tuple-element.193, f32[128,2048]{1,0:T(8,128)S(1)} %get-tuple-element.195, f32[2048]{0:T(1024)S(1)} %get-tuple-element.160, f32[2048]{0:T(1024)S(1)} %bitcast.46, ...), kind=kLoop, calls=%fused_computation.1.clone.1 | loop fusion | flops 4980480 | bytes 3195908 | tf_op jit(solution)/shard_map/while/body/eval_jaxpr/reduce_sum | solution.py:50
  457.2 5.7 %multiply_reduce_fusion.3 = (f32[128]{0:T(128)S(1)}, f32[128]{0:T(128)S(1)}) fusion(f32[128,2048]{1,0:T(8,128)S(1)} %get-tuple-element.196, f32[128,2048]{1,0:T(8,128)S(1)} %get-tuple-element.193, f32[128,2048]{1,0:T(8,128)S(1)} %get-tuple-element.195, f32[2048]{0:T(1024)S(1)} %get-tuple-element.160, f32[2048]{0:T(1024)S(1)} %bitcast.46, ...), kind=kLoop, calls=%fused_computation.1.clone.1 | loop fusion | flops 4980480 | bytes 3195908 | tf_op jit(solution)/shard_map/while/body/eval_jaxpr/reduce_sum | solution.py:50
  462.9 41.7 %psum.7 = f32[2,16,128]{2,1,0:T(8,128)} all-reduce(f32[2,16,128]{2,1,0:T(8,128)S(1)} %bitcast.54), channel_id=1, replica_groups=mesh['sect'=8,'blk'=32,'obs'=4] {'sect'}, use_global_device_ids=true, to_apply=%region_7.8 | all-reduce | flops 4096 | bytes 32768 | tf_op jit(solution)/shard_map/psum | solution.py:88
  (100 shorter events, 40.6 us)
Async XLA Ops:
  6.5 0.8 copy-start
  6.5 143.7 %reduce-scatter.2.cloned.1.call-start = ((), (), s32[]{:S(2)}) async-start(), calls=%async_computation.1 | async-start | bytes 81920 | tf_op jit(solution)/shard_map/reduce_scatter | solution.py:69
  143.7 5.0 copy-start.1
  149.6 0.7 copy-start.2
Sparse Core Ops, SparseCore 0:
  10.7 62.1 reduce-scatter.1
where the time goes:
time: 515 us; the launch traced here: 511 us
  blocking collectives  331 us (64%)
  other arithmetic  130 us (25%)
  local copies, waits for them, and re-layouts  24.3 us (5%)
  between operations  14.2 us (3%)
  loops' own time  11.7 us (2%)
    all_gather x1, blocking collectives, body(): lax.all_gather(sources, 'blk', axis=2, tiled=True)  156 us
    all_gather x1, blocking collectives, body(): lax.all_gather(geometry, 'blk', axis=2, tiled=True)  133 us
    reduce_sum x16, other arithmetic, single(): jnp.sum(spherical_decay * (cos_phase * amp_real + sin_phase * amp_imag),...  91.1 us
    psum x1, blocking collectives, body(): combined = lax.psum(pressure_part, 'sect')  41.7 us
    mul x16, other arithmetic, single(): -wavenum * thick_imag  26.2 us
    another operation x1, loops' own time, panel_field(): return lax.map(single, (wave_numbers, jnp.swapaxes(spectra, 0, 1)))  11.7 us
    mul x16, other arithmetic, single(): wavenum * load_real  11.1 us
    dynamic_slice x16, local copies, waits for them, and re-layouts, panel_field(): return lax.map(single, (wave_numbers, jnp.swapaxes(spectra, 0, 1)))  10.7 us
  transfers between devices with their start and end apart: 1, of which 0 were waited for; matrix products, arithmetic and copies ran while one was open for 1% of the time, Pallas kernels for 0%

commit v1 on v0

v1 whole, which is shorter than its diff:
```python
import math

import jax
import jax.numpy as jnp
import numpy as np
from jax import lax
from jax.experimental import pallas as pl
from jax.experimental.pallas import tpu as pltpu
from jax.sharding import PartitionSpec as P

SAMPLES = 512
FREQS = 64
P_DEV = 64
WAVE_SCALE = 0.05
FOUR_PI = 4.0 * math.pi

PARTS = 4
GROUP = FREQS // PARTS
ROWS = 2 * GROUP
STEPS = SAMPLES // PARTS
RUN = 8
LINES = 4
TILES_HERE = RUN * LINES
CHUNK = ROWS + 8
SECTIONS = 8
LANES = 128
OBS_HERE = 128
VMEM = 48 * 1024 * 1024

ALONG_Z = [[x * RUN + z for z in range(RUN)] for x in range(LINES)]
ALONG_X = [[x * RUN + z for x in range(LINES)] for z in range(RUN)]


def transform_rows():
    out = np.zeros((PARTS, PARTS, ROWS, STEPS), np.float64)
    for part in range(PARTS):
        steps = part * STEPS + np.arange(STEPS)
        for group in range(PARTS):
            bins = group * GROUP + 1 + np.arange(GROUP)
            angle = 2.0 * np.pi * ((bins[:, None] * steps[None, :]) % SAMPLES) / SAMPLES
            out[part, group, :GROUP] = np.cos(angle)
            out[part, group, GROUP:] = -np.sin(angle)
    return (out * SAMPLES**-0.5).astype(np.float32)


def spectrum_kernel(counts, rows, series, positions, normals, areas, keep, send, geometry):
    me = lax.axis_index("obs")
    live = lax.broadcasted_iota(jnp.int32, (1, P_DEV), 1) < counts[0]
    weights = areas[...] * live.astype(jnp.float32)
    weights = jnp.concatenate([weights, weights], axis=1)
    flat = series[...].reshape(2 * P_DEV, STEPS)
    for slot, flip in enumerate((0, 3, 1, 2)):
        spectra = lax.dot_general(
            rows[me, me ^ flip],
            flat,
            (((1,), (1,)), ((), ())),
            precision=lax.Precision.HIGHEST,
            preferred_element_type=jnp.float32,
        )
        target = keep if slot < 2 else send
        target[pl.ds((slot % 2) * ROWS, ROWS), :] = spectra * weights
    geometry[...] = jnp.broadcast_to(counts[0].astype(jnp.float32), (8, LANES))
    geometry[pl.ds(0, 3), :] = jnp.concatenate([positions[...], normals[...]], axis=1)


def spectrum_parts(series, positions, normals, areas, counts):
    block = jax.ShapeDtypeStruct((2 * ROWS, LANES), jnp.float32)
    whole = pl.BlockSpec(memory_space=pltpu.VMEM)
    return pl.pallas_call(
        spectrum_kernel,
        out_shape=(block, block, jax.ShapeDtypeStruct((8, LANES), jnp.float32)),
        in_specs=[pl.BlockSpec(memory_space=pltpu.SMEM)] + [whole] * 5,
        out_specs=(whole,) * 3,
        compiler_params=pltpu.CompilerParams(vmem_limit_bytes=VMEM),
    )(counts, jnp.asarray(transform_rows()), series, positions, normals, areas[None])


BLOCK = 32
SPAN = TILES_HERE * P_DEV // LANES + 1
Q_RE, Q_IM, POS = 0, GROUP, ROWS
L_RE, L_IM, NORMAL = CHUNK, CHUNK + GROUP, CHUNK + ROWS
M_RE, M_IM = 2 * CHUNK, 2 * CHUNK + GROUP
PACKED = 2 * CHUNK + ROWS


def field_kernel(observers, tiles, out, spread, packed, total, final):
    group = lax.axis_index("obs")
    lane = lax.broadcasted_iota(jnp.int32, (CHUNK, LANES), 1)

    def pack(tile, first):
        x = tiles[tile]
        count = tiles[tile, pl.ds(ROWS + 3, 1), pl.ds(0, 1)][0, 0].astype(jnp.int32)
        shift, base = first & (LANES - 1), first >> 7
        ahead = lane >= shift
        for start, x_half, turn in (
            (0, jnp.where(lane < P_DEV, x, 0.0), shift),
            (CHUNK, jnp.where(lane >= P_DEV, x, 0.0), (shift + P_DEV) & (LANES - 1)),
        ):
            turned = pltpu.roll(x_half, turn, 1)
            here = pl.ds(start, CHUNK)
            packed[base, here, :] = jnp.where(ahead, turned, packed[base, here, :])
            packed[base + 1, here, :] = jnp.where(ahead, 0.0, turned)
        return first + count

    live = lax.fori_loop(0, TILES_HERE, pack, jnp.int32(0))
    groups = (live + (LANES - 1)) >> 7

    columns = jnp.transpose(
        jnp.concatenate([observers[...], jnp.zeros((LANES - 3, OBS_HERE), jnp.float32)], axis=0)
    )
    for axis in range(3):
        spread[axis] = jnp.broadcast_to(columns[:, axis : axis + 1], (OBS_HERE, LANES))

    def clear(row, carry):
        total[row] = jnp.zeros((OBS_HERE, LANES), jnp.float32)
        return carry

    lax.fori_loop(0, ROWS, clear, 0)

    numbers = group * GROUP + 1 + lax.broadcasted_iota(jnp.int32, (GROUP, LANES), 0)
    wave = WAVE_SCALE * numbers.astype(jnp.float32)
    odd, high = (group & 1) == 1, (group & 2) == 2

    def panels(at, carry):
        packed[at, pl.ds(M_RE, GROUP), :] = packed[at, pl.ds(L_IM, GROUP), :] / wave
        packed[at, pl.ds(M_IM, GROUP), :] = -packed[at, pl.ds(L_RE, GROUP), :] / wave

        def row(number):
            return jnp.broadcast_to(packed[at, pl.ds(number, 1), :], (BLOCK, LANES))

        def block(step, inner):
            here = pl.ds(pl.multiple_of(step * BLOCK, BLOCK), BLOCK)
            d = [spread[axis, here, :] - row(POS + axis) for axis in range(3)]
            square = d[0] * d[0] + d[1] * d[1] + d[2] * d[2]
            inverse = lax.rsqrt(square)
            inverse = inverse * (1.5 - 0.5 * square * inverse * inverse)
            along = row(NORMAL) * d[0] + row(NORMAL + 1) * d[1] + row(NORMAL + 2) * d[2]
            cosine = along * inverse
            cosine_over = cosine * inverse
            theta = WAVE_SCALE * (square * inverse)
            t = theta * theta
            c1 = 1.0 + t * (-1 / 2 + t * (1 / 24 + t * (-1 / 720 + t * (1 / 40320))))
            s1 = theta * (1.0 + t * (-1 / 6 + t * (1 / 120 + t * (-1 / 5040 + t * (1 / 362880)))))
            c, s = c1, s1
            for _ in range(4):
                c, s = 1.0 - 2.0 * (s * s), 2.0 * (s * c)
            c32, s32 = 1.0 - 2.0 * (s * s), 2.0 * (s * c)
            ca, sa = jnp.where(odd, c, 1.0), jnp.where(odd, s, 0.0)
            cb, sb = jnp.where(high, c32, 1.0), jnp.where(high, s32, 0.0)
            before_re = inverse * (ca * cb - sa * sb)
            before_im = -inverse * (sa * cb + ca * sb)
            now_re = before_re * c1 + before_im * s1
            now_im = before_im * c1 - before_re * s1
            twice = 2.0 * c1
            for f in range(GROUP):
                a_re = row(Q_RE + f) + cosine * row(L_RE + f) + cosine_over * row(M_RE + f)
                a_im = row(Q_IM + f) + cosine * row(L_IM + f) + cosine_over * row(M_IM + f)
                total[f, here, :] += now_re * a_re - now_im * a_im
                total[GROUP + f, here, :] += now_re * a_im + now_im * a_re
                if f + 1 < GROUP:
                    before_re, now_re = now_re, twice * now_re - before_re
                    before_im, now_im = now_im, twice * now_im - before_im
            return inner

        return lax.fori_loop(0, OBS_HERE // BLOCK, block, carry)

    lax.fori_loop(0, groups, panels, 0)

    ones = jnp.ones((LANES, LANES), jnp.bfloat16)
    diagonal = lax.broadcasted_iota(jnp.int32, (OBS_HERE, LANES), 0) == lax.broadcasted_iota(
        jnp.int32, (OBS_HERE, LANES), 1
    )

    for i in range(ROWS):
        x = total[i]
        summed = jnp.zeros((OBS_HERE, LANES), jnp.float32)
        for _ in range(3):
            piece = x.astype(jnp.bfloat16)
            x = x - piece.astype(jnp.float32)
            summed += jnp.dot(piece, ones, preferred_element_type=jnp.float32)
        final[pl.ds(i, 1), :] = jnp.sum(jnp.where(diagonal, summed, 0.0), axis=0, keepdims=True)

    scale = wave * (1.0 / FOUR_PI)
    real = -scale * final[pl.ds(GROUP, GROUP), :]
    imag = scale * final[pl.ds(0, GROUP), :]
    for copy in range(SECTIONS):
        out[copy, pl.ds(0, GROUP), :] = real
        out[copy, pl.ds(GROUP, GROUP), :] = imag


def field(observers, tiles):
    whole = pl.BlockSpec(memory_space=pltpu.VMEM)
    return pl.pallas_call(
        field_kernel,
        out_shape=jax.ShapeDtypeStruct((SECTIONS, ROWS, OBS_HERE), jnp.float32),
        in_specs=[whole, whole],
        out_specs=whole,
        scratch_shapes=[
            pltpu.VMEM((3, OBS_HERE, LANES), jnp.float32),
            pltpu.VMEM((SPAN, PACKED, LANES), jnp.float32),
            pltpu.VMEM((ROWS, OBS_HERE, LANES), jnp.float32),
            pltpu.VMEM((ROWS, OBS_HERE), jnp.float32),
        ],
        compiler_params=pltpu.CompilerParams(vmem_limit_bytes=VMEM),
    )(observers, tiles)


def swap(x, flip):
    return lax.ppermute(x, "obs", [(i, i ^ flip) for i in range(PARTS)])


def body(series, positions, normals, areas, counts, observers):
    keep, send, geometry = spectrum_parts(series, positions, normals, areas, counts)
    pair = keep + swap(send, 1)
    sources = pair[:ROWS] + swap(pair[ROWS:], 3)
    chunk = jnp.concatenate([sources, geometry])
    tiles = lax.all_to_all(
        jnp.broadcast_to(chunk[None], (RUN, CHUNK, LANES)),
        "blk", 0, 0, tiled=True, axis_index_groups=ALONG_Z,
    )
    tiles = lax.all_to_all(
        jnp.broadcast_to(tiles[None], (LINES, RUN, CHUNK, LANES)).reshape(TILES_HERE, CHUNK, LANES),
        "blk", 0, 0, tiled=True, axis_index_groups=ALONG_X,
    )
    parts = lax.all_to_all(field(observers, tiles), "sect", 0, 0, tiled=True)
    return jnp.sum(parts, axis=0).reshape(2, GROUP, OBS_HERE)


def solution(mesh):
    placed = (
        P(None, ("sect", "blk"), "obs"),
        P(None, ("sect", "blk")),
        P(None, ("sect", "blk")),
        P(("sect", "blk")),
        P(("sect", "blk")),
        P(None, "blk"),
    )
    return jax.shard_map(
        body, mesh=mesh, in_specs=placed, out_specs=P(None, "obs", "blk"), check_vma=False
    )
```

time: 515 us -> 100 us (0.19)
  blocking collectives: 331 us -> 45.4 us
  other arithmetic: 130 us -> 0.63 us
  starting transfers between devices: 0.01 us -> 35.6 us
  local copies, waits for them, and re-layouts: 24.3 us -> 3.18 us
  between operations: 14.2 us -> 0.72 us
  Pallas kernels: 0 us -> 11.9 us
  loops' own time: 11.7 us -> 0 us
    all_gather x2 -> x0, blocking collectives: 289 us -> none  [the longest x1 156 us: body(): lax.all_gather(sources, 'blk', axis=2, tiled=True)]
    reduce_sum x17 -> x1, other arithmetic: 91.9 us -> 0.62 us  [body(): return jnp.sum(parts, axis=0).reshape(2, GROUP, OBS_HERE)]
    all_to_all x0 -> x3, blocking collectives: none -> 45.4 us  [the longest x1 17 us: body(): parts = lax.all_to_all(field(observers, tiles), 'sect', 0, 0, tiled=True)]
    psum x1 -> x0, blocking collectives: 41.7 us -> none  [body(): combined = lax.psum(pressure_part, 'sect')]
    mul x35 -> x0, other arithmetic: 37.3 us -> none  [the longest x16 26.2 us: single(): -wavenum * thick_imag]
    ppermute x0 -> x2, starting transfers between devices: none -> 35.6 us  [swap(): return lax.ppermute(x, 'obs', [(i, i ^ flip) for i in range(PARTS)])]
    pallas_call x0 -> x2, Pallas kernels: none -> 11.9 us  [the longest x1 11.4 us: field(): pl.pallas_call(field_kernel, out_shape=jax.ShapeDtypeStruct((SECTIONS, RO...]
    another operation x1 -> x0, loops' own time: 11.7 us -> none  [panel_field(): return lax.map(single, (wave_numbers, jnp.swapaxes(spectra, 0, 1)))]
  transfers between devices with their start and end apart: 1 -> 2, of which waited for: 0 -> 2; matrix products, arithmetic and copies ran while one was open for 1% -> 0% of each run, Pallas kernels for 0% -> 0%
where the time goes in v1:
time: 100 us; the launch traced here: 99.9 us
  blocking collectives  45.4 us (45%)
  starting transfers between devices  35.6 us (36%)
  Pallas kernels  11.9 us (12%)
  local copies, waits for them, and re-layouts  3.18 us (3%)
  waiting for transfers between devices  2.4 us (2%)
    ppermute x2, starting transfers between devices, swap(): return lax.ppermute(x, 'obs', [(i, i ^ flip) for i in range(PARTS)])  35.6 us
    all_to_all x1, blocking collectives, body(): parts = lax.all_to_all(field(observers, tiles), 'sect', 0, 0, tiled=True)  17 us
    all_to_all x1, blocking collectives, body(): lax.all_to_all(jnp.broadcast_to(chunk[None], (RUN, CHUNK, LANES)), 'blk',...  17 us
    all_to_all x1, blocking collectives, body(): lax.all_to_all(jnp.broadcast_to(tiles[None], (LINES, RUN, CHUNK, LANES))....  11.4 us
    pallas_call x1, Pallas kernels, field(): pl.pallas_call(field_kernel, out_shape=jax.ShapeDtypeStruct((SECTIONS, RO...  11.4 us
    unnamed x12, local copies, waits for them, and re-layouts  3.12 us
    ppermute x2, waiting for transfers between devices, swap(): return lax.ppermute(x, 'obs', [(i, i ^ flip) for i in range(PARTS)])  2.4 us
  transfers between devices with their start and end apart: 2, of which 2 were waited for; matrix products, arithmetic and copies ran while one was open for 0% of the time, Pallas kernels for 0%

profile of v1, /device:TPU:1, one launch (start us, length us, event | category | flops | bytes accessed | tf_op | source)
XLA Modules:
  0.0 99.9 jit_solution(16928643265895639571)
XLA Ops:
  0.0 0.0 copy-start.3
  0.7 0.0 copy-start.5
  0.7 0.0 copy-done.3
  0.7 0.6 copy-done.5
  1.3 0.0 copy-start
  1.3 0.9 copy-done
  2.3 0.0 copy-start.1
  2.3 0.8 copy-done.1
  3.1 0.0 copy-start.4
  3.1 0.7 copy-done.4
  3.8 0.5 shard_map.73
  4.3 16.3 %collective-permute-start = (f32[64,128]{1,0:T(8,128)S(1)}, f32[64,128]{1,0:T(8,128)S(1)}, u32[]{:S(2)}, u32[]{:S(2)}) collective-permute-start(f32[64,128]{1,0:T(8,128)S(1)} %get-tuple-element.9), channel_id=1, source_target_pairs={{0,1},{1,0},{2,3},{3,2},{4,5},{5,4},{6,7},{7,6},{8,9},{9,8},{10,11... | collective-permute-start | bytes 98312 | tf_op jit(solution)/shard_map/ppermute | solution.py:209
  20.6 1.3 %collective-permute-done = f32[64,128]{1,0:T(8,128)S(1)} collective-permute-done((f32[64,128]{1,0:T(8,128)S(1)}, f32[64,128]{1,0:T(8,128)S(1)}, u32[]{:S(2)}, u32[]{:S(2)}) %collective-permute-start) | collective-permute-done | bytes 32800 | tf_op jit(solution)/shard_map/ppermute | solution.py:209
  21.9 19.4 %collective-permute-start.1 = (f32[32,128]{1,0:T(8,128)S(1)}, f32[32,128]{1,0:T(8,128)S(1)}, u32[]{:S(2)}, u32[]{:S(2)}) collective-permute-start(f32[32,128]{1,0:T(8,128)S(1)} %slice.9), channel_id=1, source_target_pairs={{0,3},{1,2},{2,1},{3,0},{4,7},{5,6},{6,5},{7,4},{8,11},{9,10},{10,... | collective-permute-start | bytes 49160 | tf_op jit(solution)/shard_map/ppermute | solution.py:209
  41.3 1.1 %collective-permute-done.1 = f32[32,128]{1,0:T(8,128)S(1)} collective-permute-done((f32[32,128]{1,0:T(8,128)S(1)}, f32[32,128]{1,0:T(8,128)S(1)}, u32[]{:S(2)}, u32[]{:S(2)}) %collective-permute-start.1) | collective-permute-done | bytes 16416 | tf_op jit(solution)/shard_map/ppermute | solution.py:209
  42.4 17.0 %all_to_all.15 = f32[8,40,128]{2,1,0:T(8,128)S(1)} all-to-all(f32[8,40,128]{2,1,0:T(8,128)S(1)} %broadcast_in_dim.7), channel_id=1, replica_groups={{0,4,8,12,16,20,24,28},{32,36,40,44,48,52,56,60},{64,68,72,76,80,84,88,..., dimensions={0} | all-to-all | bytes 327680 | tf_op jit(solution)/shard_map/all_to_all | solution.py:217
  59.4 0.0 copy-start.2
  59.5 11.4 %all_to_all.16.tiles = f32[32,40,128]{2,1,0:T(8,128)S(1)} all-to-all(f32[32,40,128]{2,1,0:T(8,128)S(1)} %bitcast.4), channel_id=1, replica_groups={{0,32,64,96},{4,36,68,100},{8,40,72,104},{12,44,76,108},{16,48,80,112},..., dimensions={0} | all-to-all | bytes 1310720 | tf_op jit(solution)/shard_map/all_to_all | solution.py:221
  70.9 0.0 copy-done.2
  70.9 11.4 %shard_map.74 = f32[8,32,128]{2,1,0:T(8,128)S(1)} custom-call(f32[3,128]{1,0:T(4,128)S(1)} %copy-done.2, f32[32,40,128]{2,1,0:T(8,128)S(1)} %all_to_all.16.tiles), custom_call_target="tpu_custom_call" | custom-call | tf_op jit(solution)/shard_map/pallas_call | solution.py:193
  82.3 17.0 %all_to_all.17 = f32[8,32,128]{2,1,0:T(8,128)S(1)} all-to-all(f32[8,32,128]{2,1,0:T(8,128)S(1)} %shard_map.74), channel_id=1, replica_groups=mesh['sect'=8,'blk'=32,'obs'=4] {'sect'}, dimensions={0} | all-to-all | bytes 262144 | tf_op jit(solution)/shard_map/all_to_all | solution.py:225
  99.3 0.6 reduce_sum.9
  (6 shorter events, 0.1 us)
Async XLA Ops:
  0.0 0.7 copy-start.3
  0.7 0.7 copy-start.5
  1.3 0.9 copy-start
  2.3 0.8 copy-start.1
  3.1 0.7 copy-start.4
  4.3 17.6 %collective-permute-start = (f32[64,128]{1,0:T(8,128)S(1)}, f32[64,128]{1,0:T(8,128)S(1)}, u32[]{:S(2)}, u32[]{:S(2)}) collective-permute-start(f32[64,128]{1,0:T(8,128)S(1)} %get-tuple-element.9), channel_id=1, source_target_pairs={{0,1},{1,0},{2,3},{3,2},{4,5},{5,4},{6,7},{7,6},{8,9},{9,8},{10,11... | collective-permute-start | bytes 98312 | tf_op jit(solution)/shard_map/ppermute | solution.py:209
  21.9 20.5 %collective-permute-start.1 = (f32[32,128]{1,0:T(8,128)S(1)}, f32[32,128]{1,0:T(8,128)S(1)}, u32[]{:S(2)}, u32[]{:S(2)}) collective-permute-start(f32[32,128]{1,0:T(8,128)S(1)} %slice.9), channel_id=1, source_target_pairs={{0,3},{1,2},{2,1},{3,0},{4,7},{5,6},{6,5},{7,4},{8,11},{9,10},{10,... | collective-permute-start | bytes 49160 | tf_op jit(solution)/shard_map/ppermute | solution.py:209
  59.4 11.5 %copy-start.2 = (f32[3,128]{1,0:T(4,128)S(1)}, f32[3,128]{1,0:T(4,128)}, u32[]{:S(2)}) copy-start(f32[3,128]{1,0:T(4,128)} %observers.1) | copy-start | bytes 4612

commit v2 on v1

--- a/solution.py
+++ b/solution.py
@@ -43,35 +43,62 @@
     return (out * SAMPLES**-0.5).astype(np.float32)
 
 
-def spectrum_kernel(counts, rows, series, positions, normals, areas, keep, send, geometry):
+def spectrum_kernel(counts, all_rows, series, positions, normals, areas, keep, send, *scratch):
     me = lax.axis_index("obs")
+    rows, samples, centres, vectors, sizes, sems = scratch
+    copies = [
+        pltpu.make_async_copy(source, target, sems.at[i])
+        for i, (source, target) in enumerate(
+            (
+                (all_rows.at[me], rows),
+                (series, samples),
+                (areas, sizes),
+                (positions, centres),
+                (normals, vectors),
+            )
+        )
+    ]
+    for copy in copies:
+        copy.start()
+    for copy in copies:
+        copy.wait()
     live = lax.broadcasted_iota(jnp.int32, (1, P_DEV), 1) < counts[0]
-    weights = areas[...] * live.astype(jnp.float32)
+    weights = sizes[...] * live.astype(jnp.float32)
     weights = jnp.concatenate([weights, weights], axis=1)
-    flat = series[...].reshape(2 * P_DEV, STEPS)
-    for slot, flip in enumerate((0, 3, 1, 2)):
+    flat = samples[...].reshape(2 * P_DEV, STEPS)
+    for slot, flip in enumerate((1, 2, 0, 3)):
         spectra = lax.dot_general(
-            rows[me, me ^ flip],
+            rows[me ^ flip],
             flat,
             (((1,), (1,)), ((), ())),
             precision=lax.Precision.HIGHEST,
             preferred_element_type=jnp.float32,
         )
-        target = keep if slot < 2 else send
+        target = send if slot < 2 else keep
         target[pl.ds((slot % 2) * ROWS, ROWS), :] = spectra * weights
-    geometry[...] = jnp.broadcast_to(counts[0].astype(jnp.float32), (8, LANES))
-    geometry[pl.ds(0, 3), :] = jnp.concatenate([positions[...], normals[...]], axis=1)
+    keep[pl.ds(2 * ROWS, 8), :] = jnp.broadcast_to(counts[0].astype(jnp.float32), (8, LANES))
+    keep[pl.ds(2 * ROWS, 3), :] = jnp.concatenate([centres[...], vectors[...]], axis=1)
 
 
 def spectrum_parts(series, positions, normals, areas, counts):
-    block = jax.ShapeDtypeStruct((2 * ROWS, LANES), jnp.float32)
     whole = pl.BlockSpec(memory_space=pltpu.VMEM)
     return pl.pallas_call(
         spectrum_kernel,
-        out_shape=(block, block, jax.ShapeDtypeStruct((8, LANES), jnp.float32)),
-        in_specs=[pl.BlockSpec(memory_space=pltpu.SMEM)] + [whole] * 5,
-        out_specs=(whole,) * 3,
-        compiler_params=pltpu.CompilerParams(vmem_limit_bytes=VMEM),
+        out_shape=(
+            jax.ShapeDtypeStruct((2 * ROWS + 8, LANES), jnp.float32),
+            jax.ShapeDtypeStruct((2 * ROWS, LANES), jnp.float32),
+        ),
+        in_specs=[pl.BlockSpec(memory_space=pltpu.SMEM)] + [pl.BlockSpec(memory_space=pltpu.HBM)] * 5,
+        out_specs=(whole,) * 2,
+        scratch_shapes=[
+            pltpu.VMEM((PARTS, ROWS, STEPS), jnp.float32),
+            pltpu.VMEM((2, P_DEV, STEPS), jnp.float32),
+            pltpu.VMEM((3, P_DEV), jnp.float32),
+            pltpu.VMEM((3, P_DEV), jnp.float32),
+            pltpu.VMEM((1, P_DEV), jnp.float32),
+            pltpu.SemaphoreType.DMA((5,)),
+        ],
+        compiler_params=pltpu.CompilerParams(vmem_limit_bytes=60 * 1024 * 1024),
     )(counts, jnp.asarray(transform_rows()), series, positions, normals, areas[None])
 
 
@@ -86,23 +113,26 @@
 def field_kernel(observers, tiles, out, spread, packed, total, final):
     group = lax.axis_index("obs")
     lane = lax.broadcasted_iota(jnp.int32, (CHUNK, LANES), 1)
-
-    def pack(tile, first):
+    first_half = lane < P_DEV
+
+    counts = [
+        tiles[tile, pl.ds(ROWS + 3, 1), pl.ds(0, 1)][0, 0].astype(jnp.int32)
+        for tile in range(TILES_HERE)
+    ]
+    live = jnp.int32(0)
+    for tile in range(TILES_HERE):
         x = tiles[tile]
-        count = tiles[tile, pl.ds(ROWS + 3, 1), pl.ds(0, 1)][0, 0].astype(jnp.int32)
-        shift, base = first & (LANES - 1), first >> 7
+        shift, base = live & (LANES - 1), live >> 7
         ahead = lane >= shift
         for start, x_half, turn in (
-            (0, jnp.where(lane < P_DEV, x, 0.0), shift),
-            (CHUNK, jnp.where(lane >= P_DEV, x, 0.0), (shift + P_DEV) & (LANES - 1)),
+            (0, jnp.where(first_half, x, 0.0), shift),
+            (CHUNK, jnp.where(first_half, 0.0, x), (shift + P_DEV) & (LANES - 1)),
         ):
             turned = pltpu.roll(x_half, turn, 1)
             here = pl.ds(start, CHUNK)
             packed[base, here, :] = jnp.where(ahead, turned, packed[base, here, :])
             packed[base + 1, here, :] = jnp.where(ahead, 0.0, turned)
-        return first + count
-
-    live = lax.fori_loop(0, TILES_HERE, pack, jnp.int32(0))
+        live = live + counts[tile]
     groups = (live + (LANES - 1)) >> 7
 
     columns = jnp.transpose(
@@ -111,11 +141,8 @@
     for axis in range(3):
         spread[axis] = jnp.broadcast_to(columns[:, axis : axis + 1], (OBS_HERE, LANES))
 
-    def clear(row, carry):
+    for row in range(ROWS):
         total[row] = jnp.zeros((OBS_HERE, LANES), jnp.float32)
-        return carry
-
-    lax.fori_loop(0, ROWS, clear, 0)
 
     numbers = group * GROUP + 1 + lax.broadcasted_iota(jnp.int32, (GROUP, LANES), 0)
     wave = WAVE_SCALE * numbers.astype(jnp.float32)
@@ -174,7 +201,7 @@
     for i in range(ROWS):
         x = total[i]
         summed = jnp.zeros((OBS_HERE, LANES), jnp.float32)
-        for _ in range(3):
+        for _ in range(2):
             piece = x.astype(jnp.bfloat16)
             x = x - piece.astype(jnp.float32)
             summed += jnp.dot(piece, ones, preferred_element_type=jnp.float32)
@@ -205,15 +232,17 @@
     )(observers, tiles)
 
 
-def swap(x, flip):
-    return lax.ppermute(x, "obs", [(i, i ^ flip) for i in range(PARTS)])
+def from_partner(x, pairs, place):
+    both = lax.all_gather(x, "obs", axis=0, axis_index_groups=pairs)
+    return jnp.where(place == 0, both[1], both[0])
 
 
 def body(series, positions, normals, areas, counts, observers):
-    keep, send, geometry = spectrum_parts(series, positions, normals, areas, counts)
-    pair = keep + swap(send, 1)
-    sources = pair[:ROWS] + swap(pair[ROWS:], 3)
-    chunk = jnp.concatenate([sources, geometry])
+    me = lax.axis_index("obs")
+    keep, send = spectrum_parts(series, positions, normals, areas, counts)
+    pair = keep[: 2 * ROWS] + from_partner(send, [[0, 1], [2, 3]], me & 1)
+    sources = pair[:ROWS] + from_partner(pair[ROWS:], [[0, 3], [1, 2]], me >> 1)
+    chunk = jnp.concatenate([sources, keep[2 * ROWS :]])
     tiles = lax.all_to_all(
         jnp.broadcast_to(chunk[None], (RUN, CHUNK, LANES)),
         "blk", 0, 0, tiled=True, axis_index_groups=ALONG_Z,

time: 100 us -> 93 us (0.930)
  starting transfers between devices: 35.6 us -> 0 us
  blocking collectives: 45.4 us -> 80.6 us
  local copies, waits for them, and re-layouts: 3.18 us -> 0.75 us
  waiting for transfers between devices: 2.4 us -> 0 us
  Pallas kernels: 11.9 us -> 9.97 us
    all_gather x0 -> x2, blocking collectives: none -> 35.9 us  [from_partner(): both = lax.all_gather(x, 'obs', axis=0, axis_index_groups=pairs)]
    ppermute x2 -> x0, starting transfers between devices: 35.6 us -> none  [swap(): return lax.ppermute(x, 'obs', [(i, i ^ flip) for i in range(PARTS)])]
    pallas_call x1, Pallas kernels: 11.4 us -> 7.89 us  [field(): pl.pallas_call(field_kernel, out_shape=jax.ShapeDtypeStruct((SECTIONS, RO...]
    unnamed x12 -> x4, local copies, waits for them, and re-layouts: 3.12 us -> 0.01 us
    ppermute x2 -> x0, waiting for transfers between devices: 2.4 us -> none  [swap(): return lax.ppermute(x, 'obs', [(i, i ^ flip) for i in range(PARTS)])]
    pallas_call x1, Pallas kernels: 0.5 us -> 2.07 us  [spectrum_parts(): pl.pallas_call(spectrum_kernel, out_shape=(jax.ShapeDtypeStruct((2 * ROWS...]
  transfers between devices with their start and end apart: 2 -> 0, of which waited for: 2 -> 0; matrix products, arithmetic and copies ran while one was open for 0% -> 0% of each run, Pallas kernels for 0% -> 0%
where the time goes in v2:
time: 93 us; the launch traced here: 92.6 us
  blocking collectives  80.6 us (87%)
  Pallas kernels  9.97 us (11%)
    all_gather x2, blocking collectives, from_partner(): both = lax.all_gather(x, 'obs', axis=0, axis_index_groups=pairs)  35.9 us
    all_to_all x1, blocking collectives, body(): lax.all_to_all(jnp.broadcast_to(chunk[None], (RUN, CHUNK, LANES)), 'blk',...  17 us
    all_to_all x1, blocking collectives, body(): parts = lax.all_to_all(field(observers, tiles), 'sect', 0, 0, tiled=True)  16.2 us
    all_to_all x1, blocking collectives, body(): lax.all_to_all(jnp.broadcast_to(tiles[None], (LINES, RUN, CHUNK, LANES))....  11.4 us
    pallas_call x1, Pallas kernels, field(): pl.pallas_call(field_kernel, out_shape=jax.ShapeDtypeStruct((SECTIONS, RO...  7.89 us
    pallas_call x1, Pallas kernels, spectrum_parts(): pl.pallas_call(spectrum_kernel, out_shape=(jax.ShapeDtypeStruct((2 * ROWS...  2.07 us

profile of v2, /device:TPU:1, one launch (start us, length us, event | category | flops | bytes accessed | tf_op | source)
XLA Modules:
  0.0 92.6 jit_solution(384546078148570008)
XLA Ops:
  0.7 2.1 %shard_map.73 = (f32[72,128]{1,0:T(8,128)}, f32[64,128]{1,0:T(8,128)}) custom-call(s32[1]{0:T(128)S(6)} %copy.8.counts, f32[4,4,32,128]{3,2,1,0:T(8,128)} %constant.12.clone.all_rows, f32[2,64,128]{2,1,0:T(8,128)} %series.1, f32[3,64]{1,0:T(4,128)} %positions.1, f32[3,64]{1,0:T(4,128)} %normals.1, f32[1,64]{1,0:T(1,128)} %bitcast.4), custom_call_target="tpu_custom_call" | custom-call | tf_op jit(solution)/shard_map/pallas_call | solution.py:85
  2.7 0.7 slice.31
  3.4 0.0 copy-start.1
  3.4 16.7 %all-gather = f32[128,128]{1,0:T(8,128)S(1)} all-gather(f32[64,128]{1,0:T(8,128)} %get-tuple-element.8), channel_id=2, replica_groups={{0,1},{2,3},{4,5},{6,7},{8,9},{10,11},{12,13},{14,15},{16,17},{18,19},{..., dimensions={0}, use_global_device_ids=true | all-gather | bytes 98304 | tf_op jit(solution)/shard_map/all_gather | solution.py:236
  20.1 0.0 copy-done.1
  20.2 19.2 %all-gather.1 = f32[64,128]{1,0:T(8,128)S(1)} all-gather(f32[32,128]{1,0:T(8,128)S(1)} %slice.39), channel_id=3, replica_groups={{0,3},{1,2},{4,7},{5,6},{8,11},{9,10},{12,15},{13,14},{16,19},{17,18},{..., dimensions={0}, use_global_device_ids=true | all-gather | bytes 49152 | tf_op jit(solution)/shard_map/all_gather | solution.py:236
  39.4 17.0 %all_to_all.15 = f32[8,40,128]{2,1,0:T(8,128)S(1)} all-to-all(f32[8,40,128]{2,1,0:T(8,128)S(1)} %broadcast_in_dim.7), channel_id=1, replica_groups={{0,4,8,12,16,20,24,28},{32,36,40,44,48,52,56,60},{64,68,72,76,80,84,88,..., dimensions={0} | all-to-all | bytes 327680 | tf_op jit(solution)/shard_map/all_to_all | solution.py:246
  56.5 0.0 copy-start
  56.5 11.4 %all_to_all.16.tiles = f32[32,40,128]{2,1,0:T(8,128)S(1)} all-to-all(f32[32,40,128]{2,1,0:T(8,128)S(1)} %bitcast.3), channel_id=1, replica_groups={{0,32,64,96},{4,36,68,100},{8,40,72,104},{12,44,76,108},{16,48,80,112},..., dimensions={0} | all-to-all | bytes 1310720 | tf_op jit(solution)/shard_map/all_to_all | solution.py:250
  67.9 0.0 copy-done
  67.9 7.9 %shard_map.74 = f32[8,32,128]{2,1,0:T(8,128)S(1)} custom-call(f32[3,128]{1,0:T(4,128)S(1)} %copy-done, f32[32,40,128]{2,1,0:T(8,128)S(1)} %all_to_all.16.tiles), custom_call_target="tpu_custom_call" | custom-call | tf_op jit(solution)/shard_map/pallas_call | solution.py:220
  75.8 16.2 %all_to_all.17 = f32[8,32,128]{2,1,0:T(8,128)S(1)} all-to-all(f32[8,32,128]{2,1,0:T(8,128)S(1)} %shard_map.74), channel_id=1, replica_groups=mesh['sect'=8,'blk'=32,'obs'=4] {'sect'}, dimensions={0} | all-to-all | bytes 262144 | tf_op jit(solution)/shard_map/all_to_all | solution.py:254
  92.0 0.6 reduce_sum.9
  (6 shorter events, 0.1 us)
Async XLA Ops:
  3.4 16.7 %copy-start.1 = (f32[72,128]{1,0:T(8,128)S(1)}, f32[72,128]{1,0:T(8,128)}, u32[]{:S(2)}) copy-start(f32[72,128]{1,0:T(8,128)} %get-tuple-element.7) | copy-start | bytes 110596
  56.5 11.5 %copy-start = (f32[3,128]{1,0:T(4,128)S(1)}, f32[3,128]{1,0:T(4,128)}, u32[]{:S(2)}) copy-start(f32[3,128]{1,0:T(4,128)} %observers.1) | copy-start | bytes 4612

commit v3 on v2

--- a/solution.py
+++ b/solution.py
@@ -43,7 +43,7 @@
     return (out * SAMPLES**-0.5).astype(np.float32)
 
 
-def spectrum_kernel(counts, all_rows, series, positions, normals, areas, keep, send, *scratch):
+def spectrum_kernel(counts, all_rows, series, positions, normals, areas, keep, send, geometry, *scratch):
     me = lax.axis_index("obs")
     rows, samples, centres, vectors, sizes, sems = scratch
     copies = [
@@ -76,20 +76,18 @@
         )
         target = send if slot < 2 else keep
         target[pl.ds((slot % 2) * ROWS, ROWS), :] = spectra * weights
-    keep[pl.ds(2 * ROWS, 8), :] = jnp.broadcast_to(counts[0].astype(jnp.float32), (8, LANES))
-    keep[pl.ds(2 * ROWS, 3), :] = jnp.concatenate([centres[...], vectors[...]], axis=1)
+    geometry[...] = jnp.broadcast_to(counts[0].astype(jnp.float32), (8, LANES))
+    geometry[pl.ds(0, 3), :] = jnp.concatenate([centres[...], vectors[...]], axis=1)
 
 
 def spectrum_parts(series, positions, normals, areas, counts):
+    block = jax.ShapeDtypeStruct((2 * ROWS, LANES), jnp.float32)
     whole = pl.BlockSpec(memory_space=pltpu.VMEM)
     return pl.pallas_call(
         spectrum_kernel,
-        out_shape=(
-            jax.ShapeDtypeStruct((2 * ROWS + 8, LANES), jnp.float32),
-            jax.ShapeDtypeStruct((2 * ROWS, LANES), jnp.float32),
-        ),
+        out_shape=(block, block, jax.ShapeDtypeStruct((8, LANES), jnp.float32)),
         in_specs=[pl.BlockSpec(memory_space=pltpu.SMEM)] + [pl.BlockSpec(memory_space=pltpu.HBM)] * 5,
-        out_specs=(whole,) * 2,
+        out_specs=(whole,) * 3,
         scratch_shapes=[
             pltpu.VMEM((PARTS, ROWS, STEPS), jnp.float32),
             pltpu.VMEM((2, P_DEV, STEPS), jnp.float32),
@@ -98,7 +96,7 @@
             pltpu.VMEM((1, P_DEV), jnp.float32),
             pltpu.SemaphoreType.DMA((5,)),
         ],
-        compiler_params=pltpu.CompilerParams(vmem_limit_bytes=60 * 1024 * 1024),
+        compiler_params=pltpu.CompilerParams(vmem_limit_bytes=55091 * 1024),
     )(counts, jnp.asarray(transform_rows()), series, positions, normals, areas[None])
 
 
@@ -160,7 +158,6 @@
             d = [spread[axis, here, :] - row(POS + axis) for axis in range(3)]
             square = d[0] * d[0] + d[1] * d[1] + d[2] * d[2]
             inverse = lax.rsqrt(square)
-            inverse = inverse * (1.5 - 0.5 * square * inverse * inverse)
             along = row(NORMAL) * d[0] + row(NORMAL + 1) * d[1] + row(NORMAL + 2) * d[2]
             cosine = along * inverse
             cosine_over = cosine * inverse
@@ -239,10 +236,10 @@
 
 def body(series, positions, normals, areas, counts, observers):
     me = lax.axis_index("obs")
-    keep, send = spectrum_parts(series, positions, normals, areas, counts)
-    pair = keep[: 2 * ROWS] + from_partner(send, [[0, 1], [2, 3]], me & 1)
+    keep, send, geometry = spectrum_parts(series, positions, normals, areas, counts)
+    pair = keep + from_partner(send, [[0, 1], [2, 3]], me & 1)
     sources = pair[:ROWS] + from_partner(pair[ROWS:], [[0, 3], [1, 2]], me >> 1)
-    chunk = jnp.concatenate([sources, keep[2 * ROWS :]])
+    chunk = jnp.concatenate([sources, geometry])
     tiles = lax.all_to_all(
         jnp.broadcast_to(chunk[None], (RUN, CHUNK, LANES)),
         "blk", 0, 0, tiled=True, axis_index_groups=ALONG_Z,

time: 93 us -> 91.8 us (0.987)
  blocking collectives: 80.6 us -> 79.3 us
where the time goes in v3:
time: 91.8 us; the launch traced here: 91.5 us
  blocking collectives  79.3 us (86%)
  Pallas kernels  10.1 us (11%)
    all_gather x2, blocking collectives, from_partner(): both = lax.all_gather(x, 'obs', axis=0, axis_index_groups=pairs)  35.6 us
    all_to_all x1, blocking collectives, body(): lax.all_to_all(jnp.broadcast_to(chunk[None], (RUN, CHUNK, LANES)), 'blk',...  17 us
    all_to_all x1, blocking collectives, body(): parts = lax.all_to_all(field(observers, tiles), 'sect', 0, 0, tiled=True)  15.3 us
    all_to_all x1, blocking collectives, body(): lax.all_to_all(jnp.broadcast_to(tiles[None], (LINES, RUN, CHUNK, LANES))....  11.4 us
    pallas_call x1, Pallas kernels, field(): pl.pallas_call(field_kernel, out_shape=jax.ShapeDtypeStruct((SECTIONS, RO...  8.66 us

profile of v3, /device:TPU:1, one launch (start us, length us, event | category | flops | bytes accessed | tf_op | source)
XLA Modules:
  0.0 91.5 jit_solution(13302981307698703614)
XLA Ops:
  0.0 0.0 copy-start.2
  0.0 0.0 copy-start.1
  0.7 0.0 copy-start.3
  0.7 0.0 copy-done.2
  0.7 0.0 copy-done.1
  0.7 0.6 copy-done.3
  1.3 1.4 %shard_map.73 = (f32[64,128]{1,0:T(8,128)S(1)}, f32[64,128]{1,0:T(8,128)S(1)}, f32[8,128]{1,0:T(8,128)S(1)}) custom-call(s32[1]{0:T(128)S(6)} %copy.8.counts, f32[4,4,32,128]{3,2,1,0:T(8,128)} %constant.12.clone.all_rows, f32[2,64,128]{2,1,0:T(8,128)} %series.1, f32[3,64]{1,0:T(4,128)S(1)} %copy-done.1, f32[3,64]{1,0:T(4,128)S(1)} %copy-done.2, ...), custom_call_target="tpu_custom_call" | custom-call | tf_op jit(solution)/shard_map/pallas_call | solution.py:86
  2.8 16.3 %all-gather = f32[128,128]{1,0:T(8,128)S(1)} all-gather(f32[64,128]{1,0:T(8,128)S(1)} %get-tuple-element.9), channel_id=2, replica_groups={{0,1},{2,3},{4,5},{6,7},{8,9},{10,11},{12,13},{14,15},{16,17},{18,19},{..., dimensions={0}, use_global_device_ids=true | all-gather | bytes 98304 | tf_op jit(solution)/shard_map/all_gather | solution.py:233
  19.1 19.3 %all-gather.1 = f32[64,128]{1,0:T(8,128)S(1)} all-gather(f32[32,128]{1,0:T(8,128)S(1)} %slice.31), channel_id=3, replica_groups={{0,3},{1,2},{4,7},{5,6},{8,11},{9,10},{12,15},{13,14},{16,19},{17,18},{..., dimensions={0}, use_global_device_ids=true | all-gather | bytes 49152 | tf_op jit(solution)/shard_map/all_gather | solution.py:233
  38.4 17.0 %all_to_all.15 = f32[8,40,128]{2,1,0:T(8,128)S(1)} all-to-all(f32[8,40,128]{2,1,0:T(8,128)S(1)} %broadcast_in_dim.7), channel_id=1, replica_groups={{0,4,8,12,16,20,24,28},{32,36,40,44,48,52,56,60},{64,68,72,76,80,84,88,..., dimensions={0} | all-to-all | bytes 327680 | tf_op jit(solution)/shard_map/all_to_all | solution.py:243
  55.5 0.0 copy-start
  55.5 11.4 %all_to_all.16.tiles = f32[32,40,128]{2,1,0:T(8,128)S(1)} all-to-all(f32[32,40,128]{2,1,0:T(8,128)S(1)} %bitcast.4), channel_id=1, replica_groups={{0,32,64,96},{4,36,68,100},{8,40,72,104},{12,44,76,108},{16,48,80,112},..., dimensions={0} | all-to-all | bytes 1310720 | tf_op jit(solution)/shard_map/all_to_all | solution.py:247
  67.0 0.0 copy-done
  67.0 8.7 %shard_map.74 = f32[8,32,128]{2,1,0:T(8,128)S(1)} custom-call(f32[3,128]{1,0:T(4,128)S(1)} %copy-done, f32[32,40,128]{2,1,0:T(8,128)S(1)} %all_to_all.16.tiles), custom_call_target="tpu_custom_call" | custom-call | tf_op jit(solution)/shard_map/pallas_call | solution.py:217
  75.6 15.3 %all_to_all.17 = f32[8,32,128]{2,1,0:T(8,128)S(1)} all-to-all(f32[8,32,128]{2,1,0:T(8,128)S(1)} %shard_map.74), channel_id=1, replica_groups=mesh['sect'=8,'blk'=32,'obs'=4] {'sect'}, dimensions={0} | all-to-all | bytes 262144 | tf_op jit(solution)/shard_map/all_to_all | solution.py:251
  90.9 0.6 reduce_sum.9
  (6 shorter events, 0.1 us)
Async XLA Ops:
  0.0 0.7 copy-start.2
  0.0 0.7 copy-start.1
  0.7 0.7 copy-start.3
  55.5 11.5 %copy-start = (f32[3,128]{1,0:T(4,128)S(1)}, f32[3,128]{1,0:T(4,128)}, u32[]{:S(2)}) copy-start(f32[3,128]{1,0:T(4,128)} %observers.1) | copy-start | bytes 4612

commit v4 on v3

--- a/solution.py
+++ b/solution.py
@@ -43,18 +43,15 @@
     return (out * SAMPLES**-0.5).astype(np.float32)
 
 
-def spectrum_kernel(counts, all_rows, series, positions, normals, areas, keep, send, geometry, *scratch):
+def spectrum_kernel(counts, all_rows, series, panels, keep, send, geometry, *scratch):
     me = lax.axis_index("obs")
-    rows, samples, centres, vectors, sizes, sems = scratch
+    rows, samples, sems = scratch
     copies = [
         pltpu.make_async_copy(source, target, sems.at[i])
         for i, (source, target) in enumerate(
             (
                 (all_rows.at[me], rows),
                 (series, samples),
-                (areas, sizes),
-                (positions, centres),
-                (normals, vectors),
             )
         )
     ]
@@ -63,7 +60,7 @@
     for copy in copies:
         copy.wait()
     live = lax.broadcasted_iota(jnp.int32, (1, P_DEV), 1) < counts[0]
-    weights = sizes[...] * live.astype(jnp.float32)
+    weights = panels[pl.ds(6, 1), :] * live.astype(jnp.float32)
     weights = jnp.concatenate([weights, weights], axis=1)
     flat = samples[...].reshape(2 * P_DEV, STEPS)
     for slot, flip in enumerate((1, 2, 0, 3)):
@@ -77,48 +74,48 @@
         target = send if slot < 2 else keep
         target[pl.ds((slot % 2) * ROWS, ROWS), :] = spectra * weights
     geometry[...] = jnp.broadcast_to(counts[0].astype(jnp.float32), (8, LANES))
-    geometry[pl.ds(0, 3), :] = jnp.concatenate([centres[...], vectors[...]], axis=1)
+    geometry[pl.ds(0, 3), :] = jnp.concatenate(
+        [panels[pl.ds(0, 3), :], panels[pl.ds(3, 3), :]], axis=1
+    )
 
 
 def spectrum_parts(series, positions, normals, areas, counts):
     block = jax.ShapeDtypeStruct((2 * ROWS, LANES), jnp.float32)
     whole = pl.BlockSpec(memory_space=pltpu.VMEM)
+    panels = jnp.concatenate([positions, normals, areas[None], areas[None]])
     return pl.pallas_call(
         spectrum_kernel,
         out_shape=(block, block, jax.ShapeDtypeStruct((8, LANES), jnp.float32)),
-        in_specs=[pl.BlockSpec(memory_space=pltpu.SMEM)] + [pl.BlockSpec(memory_space=pltpu.HBM)] * 5,
+        in_specs=[pl.BlockSpec(memory_space=pltpu.SMEM)]
+        + [pl.BlockSpec(memory_space=pltpu.HBM)] * 2
+        + [whole],
         out_specs=(whole,) * 3,
         scratch_shapes=[
             pltpu.VMEM((PARTS, ROWS, STEPS), jnp.float32),
             pltpu.VMEM((2, P_DEV, STEPS), jnp.float32),
-            pltpu.VMEM((3, P_DEV), jnp.float32),
-            pltpu.VMEM((3, P_DEV), jnp.float32),
-            pltpu.VMEM((1, P_DEV), jnp.float32),
-            pltpu.SemaphoreType.DMA((5,)),
+            pltpu.SemaphoreType.DMA((2,)),
         ],
-        compiler_params=pltpu.CompilerParams(vmem_limit_bytes=55091 * 1024),
-    )(counts, jnp.asarray(transform_rows()), series, positions, normals, areas[None])
+        compiler_params=pltpu.CompilerParams(vmem_limit_bytes=55130 * 1024),
+    )(counts, jnp.asarray(transform_rows()), series, panels)
 
 
 BLOCK = 32
-SPAN = TILES_HERE * P_DEV // LANES + 1
 Q_RE, Q_IM, POS = 0, GROUP, ROWS
 L_RE, L_IM, NORMAL = CHUNK, CHUNK + GROUP, CHUNK + ROWS
 M_RE, M_IM = 2 * CHUNK, 2 * CHUNK + GROUP
 PACKED = 2 * CHUNK + ROWS
 
 
-def field_kernel(observers, tiles, out, spread, packed, total, final):
+def add_tiles(observers, tiles, chosen, spread, packed, total):
     group = lax.axis_index("obs")
     lane = lax.broadcasted_iota(jnp.int32, (CHUNK, LANES), 1)
     first_half = lane < P_DEV
 
     counts = [
-        tiles[tile, pl.ds(ROWS + 3, 1), pl.ds(0, 1)][0, 0].astype(jnp.int32)
-        for tile in range(TILES_HERE)
+        tiles[tile, pl.ds(ROWS + 3, 1), pl.ds(0, 1)][0, 0].astype(jnp.int32) for tile in chosen
     ]
     live = jnp.int32(0)
-    for tile in range(TILES_HERE):
+    for tile, count in zip(chosen, counts):
         x = tiles[tile]
         shift, base = live & (LANES - 1), live >> 7
         ahead = lane >= shift
@@ -130,7 +127,7 @@
             here = pl.ds(start, CHUNK)
             packed[base, here, :] = jnp.where(ahead, turned, packed[base, here, :])
             packed[base + 1, here, :] = jnp.where(ahead, 0.0, turned)
-        live = live + counts[tile]
+        live = live + count
     groups = (live + (LANES - 1)) >> 7
 
     columns = jnp.transpose(
@@ -138,9 +135,6 @@
     )
     for axis in range(3):
         spread[axis] = jnp.broadcast_to(columns[:, axis : axis + 1], (OBS_HERE, LANES))
-
-    for row in range(ROWS):
-        total[row] = jnp.zeros((OBS_HERE, LANES), jnp.float32)
 
     numbers = group * GROUP + 1 + lax.broadcasted_iota(jnp.int32, (GROUP, LANES), 0)
     wave = WAVE_SCALE * numbers.astype(jnp.float32)
@@ -190,6 +184,25 @@
 
     lax.fori_loop(0, groups, panels, 0)
 
+
+def own_kernel(observers, tiles, total, spread, packed):
+    for row in range(ROWS):
+        total[row] = jnp.zeros((OBS_HERE, LANES), jnp.float32)
+    add_tiles(observers, tiles, list(range(RUN)), spread, packed, total)
+
+
+def other_kernel(observers, tiles, begun, out, spread, packed, total, final):
+    line = lax.axis_index("blk") >> 3
+    chosen = [
+        ((line + step) & (LINES - 1)) * RUN + tile for step in range(1, LINES) for tile in range(RUN)
+    ]
+    for row in range(ROWS):
+        total[row] = begun[row]
+    add_tiles(observers, tiles, chosen, spread, packed, total)
+
+    wave = WAVE_SCALE * (
+        lax.axis_index("obs") * GROUP + 1 + lax.broadcasted_iota(jnp.int32, (GROUP, LANES), 0)
+    ).astype(jnp.float32)
     ones = jnp.ones((LANES, LANES), jnp.bfloat16)
     diagonal = lax.broadcasted_iota(jnp.int32, (OBS_HERE, LANES), 0) == lax.broadcasted_iota(
         jnp.int32, (OBS_HERE, LANES), 1
@@ -212,21 +225,39 @@
         out[copy, pl.ds(GROUP, GROUP), :] = imag
 
 
-def field(observers, tiles):
-    whole = pl.BlockSpec(memory_space=pltpu.VMEM)
+WHOLE = pl.BlockSpec(memory_space=pltpu.VMEM)
+TOTAL = (ROWS, OBS_HERE, LANES)
+
+
+def shared_scratch(tiles):
+    return [
+        pltpu.VMEM((3, OBS_HERE, LANES), jnp.float32),
+        pltpu.VMEM((tiles * P_DEV // LANES + 1, PACKED, LANES), jnp.float32),
+    ]
+
+
+def field_of_own(observers, tiles):
     return pl.pallas_call(
-        field_kernel,
+        own_kernel,
+        out_shape=jax.ShapeDtypeStruct(TOTAL, jnp.float32),
+        in_specs=[WHOLE] * 2,
+        out_specs=WHOLE,
+        scratch_shapes=shared_scratch(RUN),
+        compiler_params=pltpu.CompilerParams(vmem_limit_bytes=24 * 1024 * 1024),
+        cost_estimate=pl.CostEstimate(flops=1 << 30, bytes_accessed=1 << 22, transcendentals=0),
+    )(observers, tiles)
+
+
+def field_of_others(observers, tiles, begun):
+    return pl.pallas_call(
+        other_kernel,
         out_shape=jax.ShapeDtypeStruct((SECTIONS, ROWS, OBS_HERE), jnp.float32),
-        in_specs=[whole, whole],
-        out_specs=whole,
-        scratch_shapes=[
-            pltpu.VMEM((3, OBS_HERE, LANES), jnp.float32),
-            pltpu.VMEM((SPAN, PACKED, LANES), jnp.float32),
-            pltpu.VMEM((ROWS, OBS_HERE, LANES), jnp.float32),
-            pltpu.VMEM((ROWS, OBS_HERE), jnp.float32),
-        ],
-        compiler_params=pltpu.CompilerParams(vmem_limit_bytes=VMEM),
-    )(observers, tiles)
+        in_specs=[WHOLE] * 3,
+        out_specs=WHOLE,
+        scratch_shapes=shared_scratch(TILES_HERE - RUN)
+        + [pltpu.VMEM(TOTAL, jnp.float32), pltpu.VMEM((ROWS, OBS_HERE), jnp.float32)],
+        compiler_params=pltpu.CompilerParams(vmem_limit_bytes=24 * 1024 * 1024),
+    )(observers, tiles, begun)
 
 
 def from_partner(x, pairs, place):
@@ -240,15 +271,16 @@
     pair = keep + from_partner(send, [[0, 1], [2, 3]], me & 1)
     sources = pair[:ROWS] + from_partner(pair[ROWS:], [[0, 3], [1, 2]], me >> 1)
     chunk = jnp.concatenate([sources, geometry])
-    tiles = lax.all_to_all(
+    own = lax.all_to_all(
         jnp.broadcast_to(chunk[None], (RUN, CHUNK, LANES)),
         "blk", 0, 0, tiled=True, axis_index_groups=ALONG_Z,
     )
     tiles = lax.all_to_all(
-        jnp.broadcast_to(tiles[None], (LINES, RUN, CHUNK, LANES)).reshape(TILES_HERE, CHUNK, LANES),
+        jnp.broadcast_to(own[None], (LINES, RUN, CHUNK, LANES)).reshape(TILES_HERE, CHUNK, LANES),
         "blk", 0, 0, tiled=True, axis_index_groups=ALONG_X,
     )
-    parts = lax.all_to_all(field(observers, tiles), "sect", 0, 0, tiled=True)
+    begun = field_of_own(observers, own)
+    parts = lax.all_to_all(field_of_others(observers, tiles, begun), "sect", 0, 0, tiled=True)
     return jnp.sum(parts, axis=0).reshape(2, GROUP, OBS_HERE)
 
 

time: 91.8 us -> 92 us (level)
  blocking collectives: 79.3 us -> 67.9 us
  waiting for transfers between devices: 0 us -> 4.57 us
  starting transfers between devices: 0 us -> 4.01 us
  Pallas kernels: 10.1 us -> 12.2 us
    all_to_all x2 -> x1, blocking collectives: 26.7 us -> 15.3 us  [body(): lax.all_to_all(field_of_others(observers, tiles, begun), 'sect', 0, 0, ti...]
    all_to_all x0 -> x1, waiting for transfers between devices: none -> 4.57 us  [body(): lax.all_to_all(jnp.broadcast_to(own[None], (LINES, RUN, CHUNK, LANES)).re...]
    all_to_all x0 -> x1, starting transfers between devices: none -> 4.01 us  [body(): lax.all_to_all(jnp.broadcast_to(own[None], (LINES, RUN, CHUNK, LANES)).re...]
    pallas_call x1 -> x2, Pallas kernels: 8.66 us -> 10.8 us  [the longest x1 7.74 us: field_of_others(): pl.pallas_call(other_kernel, out_shape=jax.ShapeDtypeStruct((SECTIONS, RO...]
  transfers between devices with their start and end apart: 0 -> 1, of which waited for: 0 -> 1; matrix products, arithmetic and copies ran while one was open for 0% -> 0% of each run, Pallas kernels for 0% -> 3%
where the time goes in v4:
time: 92 us; the launch traced here: 91.7 us
  blocking collectives  67.9 us (74%)
  Pallas kernels  12.2 us (13%)
  waiting for transfers between devices  4.57 us (5%)
  starting transfers between devices  4.01 us (4%)
  other arithmetic  1.38 us (2%)
    all_gather x2, blocking collectives, from_partner(): both = lax.all_gather(x, 'obs', axis=0, axis_index_groups=pairs)  35.6 us
    all_to_all x1, blocking collectives, body(): lax.all_to_all(jnp.broadcast_to(chunk[None], (RUN, CHUNK, LANES)), 'blk',...  17 us
    all_to_all x1, blocking collectives, body(): lax.all_to_all(field_of_others(observers, tiles, begun), 'sect', 0, 0, ti...  15.3 us
    pallas_call x1, Pallas kernels, field_of_others(): pl.pallas_call(other_kernel, out_shape=jax.ShapeDtypeStruct((SECTIONS, RO...  7.74 us
    all_to_all x1, waiting for transfers between devices, body(): lax.all_to_all(jnp.broadcast_to(own[None], (LINES, RUN, CHUNK, LANES)).re...  4.57 us
    all_to_all x1, starting transfers between devices, body(): lax.all_to_all(jnp.broadcast_to(own[None], (LINES, RUN, CHUNK, LANES)).re...  4.01 us
    pallas_call x1, Pallas kernels, field_of_own(): pl.pallas_call(own_kernel, out_shape=jax.ShapeDtypeStruct(TOTAL, jnp.floa...  3.06 us
  transfers between devices with their start and end apart: 1, of which 1 were waited for; matrix products, arithmetic and copies ran while one was open for 0% of the time, Pallas kernels for 3%

profile of v4, /device:TPU:1, one launch (start us, length us, event | category | flops | bytes accessed | tf_op | source)
XLA Modules:
  0.0 91.7 jit_solution(11724645437879742264)
XLA Ops:
  0.0 0.0 copy-start
  0.7 0.7 pad_maximum_fusion.1.panels
  1.4 1.4 %shard_map.73 = (f32[64,128]{1,0:T(8,128)S(1)}, f32[64,128]{1,0:T(8,128)S(1)}, f32[8,128]{1,0:T(8,128)S(1)}) custom-call(s32[1]{0:T(128)S(6)} %copy.8.counts, f32[4,4,32,128]{3,2,1,0:T(8,128)} %constant.12.clone.all_rows, f32[2,64,128]{2,1,0:T(8,128)} %series.1, f32[8,64]{1,0:T(8,128)S(1)} %pad_maximum_fusion.1.panels), custom_call_target="tpu_custom_call" | custom-call | tf_op jit(solution)/shard_map/pallas_call | solution.py:86
  2.8 16.3 %all-gather = f32[128,128]{1,0:T(8,128)S(1)} all-gather(f32[64,128]{1,0:T(8,128)S(1)} %get-tuple-element.9), channel_id=2, replica_groups={{0,1},{2,3},{4,5},{6,7},{8,9},{10,11},{12,13},{14,15},{16,17},{18,19},{..., dimensions={0}, use_global_device_ids=true | all-gather | bytes 98304 | tf_op jit(solution)/shard_map/all_gather | solution.py:264
  19.2 19.3 %all-gather.1 = f32[64,128]{1,0:T(8,128)S(1)} all-gather(f32[32,128]{1,0:T(8,128)S(1)} %slice.31), channel_id=3, replica_groups={{0,3},{1,2},{4,7},{5,6},{8,11},{9,10},{12,15},{13,14},{16,19},{17,18},{..., dimensions={0}, use_global_device_ids=true | all-gather | bytes 49152 | tf_op jit(solution)/shard_map/all_gather | solution.py:264
  38.5 17.0 %all_to_all.15.tiles = f32[8,40,128]{2,1,0:T(8,128)S(1)} all-to-all(f32[8,40,128]{2,1,0:T(8,128)S(1)} %broadcast_in_dim.7), channel_id=1, replica_groups={{0,4,8,12,16,20,24,28},{32,36,40,44,48,52,56,60},{64,68,72,76,80,84,88,..., dimensions={0} | all-to-all | bytes 327680 | tf_op jit(solution)/shard_map/all_to_all | solution.py:274
  55.5 0.9 broadcast_in_dim.8
  56.4 4.0 %all-to-all-start.1 = ((f32[32,40,128]{2,1,0:T(8,128)}), f32[32,40,128]{2,1,0:T(8,128)S(1)}, u32[]{:S(2)}, u32[]{:S(2)}) async-start(f32[32,40,128]{2,1,0:T(8,128)} %bitcast.1), calls=%async_computation.1 | async-start | bytes 1310720 | tf_op jit(solution)/shard_map/all_to_all | solution.py:278
  60.4 0.0 copy-done
  60.4 3.1 %shard_map.74.begun = f32[32,128,128]{2,1,0:T(8,128)S(1)} custom-call(f32[3,128]{1,0:T(4,128)S(1)} %copy-done, f32[8,40,128]{2,1,0:T(8,128)S(1)} %all_to_all.15.tiles), custom_call_target="tpu_custom_call" | custom-call | flops 1073741824 | bytes 4194304 | tf_op jit(solution)/shard_map/pallas_call | solution.py:240
  63.5 4.6 %all-to-all-done.1.tiles = f32[32,40,128]{2,1,0:T(8,128)S(1)} async-done(((f32[32,40,128]{2,1,0:T(8,128)}), f32[32,40,128]{2,1,0:T(8,128)S(1)}, u32[]{:S(2)}, u32[]{:S(2)}) %all-to-all-start.1) | async-done | bytes 655392 | tf_op jit(solution)/shard_map/all_to_all | solution.py:278
  68.0 7.7 %shard_map.75 = f32[8,32,128]{2,1,0:T(8,128)S(1)} custom-call(f32[3,128]{1,0:T(4,128)S(1)} %copy-done, f32[32,40,128]{2,1,0:T(8,128)S(1)} %all-to-all-done.1.tiles, f32[32,128,128]{2,1,0:T(8,128)S(1)} %shard_map.74.begun), custom_call_target="tpu_custom_call" | custom-call | tf_op jit(solution)/shard_map/pallas_call | solution.py:252
  75.8 15.3 %all_to_all.16 = f32[8,32,128]{2,1,0:T(8,128)S(1)} all-to-all(f32[8,32,128]{2,1,0:T(8,128)S(1)} %shard_map.75), channel_id=1, replica_groups=mesh['sect'=8,'blk'=32,'obs'=4] {'sect'}, dimensions={0} | all-to-all | bytes 262144 | tf_op jit(solution)/shard_map/all_to_all | solution.py:283
  91.1 0.6 reduce_sum.9
  (5 shorter events, 0.0 us)
Async XLA Ops:
  0.0 60.4 %copy-start = (f32[3,128]{1,0:T(4,128)S(1)}, f32[3,128]{1,0:T(4,128)}, u32[]{:S(2)}) copy-start(f32[3,128]{1,0:T(4,128)} %observers.3) | copy-start | bytes 4612
  56.4 11.6 %all-to-all-start.1 = ((f32[32,40,128]{2,1,0:T(8,128)}), f32[32,40,128]{2,1,0:T(8,128)S(1)}, u32[]{:S(2)}, u32[]{:S(2)}) async-start(f32[32,40,128]{2,1,0:T(8,128)} %bitcast.1), calls=%async_computation.1 | async-start | bytes 1310720 | tf_op jit(solution)/shard_map/all_to_all | solution.py:278

commit v5 on v4

--- a/solution.py
+++ b/solution.py
@@ -106,7 +106,7 @@
 PACKED = 2 * CHUNK + ROWS
 
 
-def add_tiles(observers, tiles, chosen, spread, packed, total):
+def add_tiles(tiles, chosen, spread, packed, total):
     group = lax.axis_index("obs")
     lane = lax.broadcasted_iota(jnp.int32, (CHUNK, LANES), 1)
     first_half = lane < P_DEV
@@ -129,12 +129,6 @@
             packed[base + 1, here, :] = jnp.where(ahead, 0.0, turned)
         live = live + count
     groups = (live + (LANES - 1)) >> 7
-
-    columns = jnp.transpose(
-        jnp.concatenate([observers[...], jnp.zeros((LANES - 3, OBS_HERE), jnp.float32)], axis=0)
-    )
-    for axis in range(3):
-        spread[axis] = jnp.broadcast_to(columns[:, axis : axis + 1], (OBS_HERE, LANES))
 
     numbers = group * GROUP + 1 + lax.broadcasted_iota(jnp.int32, (GROUP, LANES), 0)
     wave = WAVE_SCALE * numbers.astype(jnp.float32)
@@ -186,19 +180,25 @@
 
 
 def own_kernel(observers, tiles, total, spread, packed):
+    columns = jnp.transpose(
+        jnp.concatenate([observers[...], jnp.zeros((LANES - 3, OBS_HERE), jnp.float32)], axis=0)
+    )
+    for axis in range(3):
+        spread[axis] = jnp.broadcast_to(columns[:, axis : axis + 1], (OBS_HERE, LANES))
+
     for row in range(ROWS):
         total[row] = jnp.zeros((OBS_HERE, LANES), jnp.float32)
-    add_tiles(observers, tiles, list(range(RUN)), spread, packed, total)
-
-
-def other_kernel(observers, tiles, begun, out, spread, packed, total, final):
+    add_tiles(tiles, list(range(RUN)), spread, packed, total)
+
+
+def other_kernel(tiles, begun, spread, out, packed, total, final):
     line = lax.axis_index("blk") >> 3
     chosen = [
         ((line + step) & (LINES - 1)) * RUN + tile for step in range(1, LINES) for tile in range(RUN)
     ]
     for row in range(ROWS):
         total[row] = begun[row]
-    add_tiles(observers, tiles, chosen, spread, packed, total)
+    add_tiles(tiles, chosen, spread, packed, total)
 
     wave = WAVE_SCALE * (
         lax.axis_index("obs") * GROUP + 1 + lax.broadcasted_iota(jnp.int32, (GROUP, LANES), 0)
@@ -231,7 +231,6 @@
 
 def shared_scratch(tiles):
     return [
-        pltpu.VMEM((3, OBS_HERE, LANES), jnp.float32),
         pltpu.VMEM((tiles * P_DEV // LANES + 1, PACKED, LANES), jnp.float32),
     ]
 
@@ -239,16 +238,19 @@
 def field_of_own(observers, tiles):
     return pl.pallas_call(
         own_kernel,
-        out_shape=jax.ShapeDtypeStruct(TOTAL, jnp.float32),
+        out_shape=(
+            jax.ShapeDtypeStruct(TOTAL, jnp.float32),
+            jax.ShapeDtypeStruct((3, OBS_HERE, LANES), jnp.float32),
+        ),
         in_specs=[WHOLE] * 2,
-        out_specs=WHOLE,
+        out_specs=(WHOLE,) * 2,
         scratch_shapes=shared_scratch(RUN),
         compiler_params=pltpu.CompilerParams(vmem_limit_bytes=24 * 1024 * 1024),
         cost_estimate=pl.CostEstimate(flops=1 << 30, bytes_accessed=1 << 22, transcendentals=0),
     )(observers, tiles)
 
 
-def field_of_others(observers, tiles, begun):
+def field_of_others(tiles, begun, spread):
     return pl.pallas_call(
         other_kernel,
         out_shape=jax.ShapeDtypeStruct((SECTIONS, ROWS, OBS_HERE), jnp.float32),
@@ -257,7 +259,7 @@
         scratch_shapes=shared_scratch(TILES_HERE - RUN)
         + [pltpu.VMEM(TOTAL, jnp.float32), pltpu.VMEM((ROWS, OBS_HERE), jnp.float32)],
         compiler_params=pltpu.CompilerParams(vmem_limit_bytes=24 * 1024 * 1024),
-    )(observers, tiles, begun)
+    )(tiles, begun, spread)
 
 
 def from_partner(x, pairs, place):
@@ -279,8 +281,8 @@
         jnp.broadcast_to(own[None], (LINES, RUN, CHUNK, LANES)).reshape(TILES_HERE, CHUNK, LANES),
         "blk", 0, 0, tiled=True, axis_index_groups=ALONG_X,
     )
-    begun = field_of_own(observers, own)
-    parts = lax.all_to_all(field_of_others(observers, tiles, begun), "sect", 0, 0, tiled=True)
+    begun, spread = field_of_own(observers, own)
+    parts = lax.all_to_all(field_of_others(tiles, begun, spread), "sect", 0, 0, tiled=True)
     return jnp.sum(parts, axis=0).reshape(2, GROUP, OBS_HERE)
 
 

time: 92 us -> 92.4 us (level)
  no operation moved by 1% of the time
where the time goes in v5:
time: 92.4 us; the launch traced here: 92.5 us
  blocking collectives  68.8 us (74%)
  Pallas kernels  12.2 us (13%)
  waiting for transfers between devices  4.52 us (5%)
  starting transfers between devices  4.01 us (4%)
  other arithmetic  1.38 us (1%)
    all_gather x2, blocking collectives, from_partner(): both = lax.all_gather(x, 'obs', axis=0, axis_index_groups=pairs)  35.6 us
    all_to_all x1, blocking collectives, body(): lax.all_to_all(jnp.broadcast_to(chunk[None], (RUN, CHUNK, LANES)), 'blk',...  17 us
    all_to_all x1, blocking collectives, body(): lax.all_to_all(field_of_others(tiles, begun, spread), 'sect', 0, 0, tiled...  16.2 us
    pallas_call x1, Pallas kernels, field_of_others(): pl.pallas_call(other_kernel, out_shape=jax.ShapeDtypeStruct((SECTIONS, RO...  7.68 us
    all_to_all x1, waiting for transfers between devices, body(): lax.all_to_all(jnp.broadcast_to(own[None], (LINES, RUN, CHUNK, LANES)).re...  4.52 us
    all_to_all x1, starting transfers between devices, body(): lax.all_to_all(jnp.broadcast_to(own[None], (LINES, RUN, CHUNK, LANES)).re...  4.01 us
    pallas_call x1, Pallas kernels, field_of_own(): pl.pallas_call(own_kernel, out_shape=(jax.ShapeDtypeStruct(TOTAL, jnp.flo...  3.1 us
  transfers between devices with their start and end apart: 1, of which 1 were waited for; matrix products, arithmetic and copies ran while one was open for 0% of the time, Pallas kernels for 3%

profile of v5, /device:TPU:1, one launch (start us, length us, event | category | flops | bytes accessed | tf_op | source)
XLA Modules:
  0.0 92.5 jit_solution(2965861541420810209)
XLA Ops:
  0.0 0.0 copy-start
  0.7 0.7 pad_maximum_fusion.1.panels
  1.4 1.4 %shard_map.73 = (f32[64,128]{1,0:T(8,128)S(1)}, f32[64,128]{1,0:T(8,128)S(1)}, f32[8,128]{1,0:T(8,128)S(1)}) custom-call(s32[1]{0:T(128)S(6)} %copy.8.counts, f32[4,4,32,128]{3,2,1,0:T(8,128)} %constant.12.clone.all_rows, f32[2,64,128]{2,1,0:T(8,128)} %series.1, f32[8,64]{1,0:T(8,128)S(1)} %pad_maximum_fusion.1.panels), custom_call_target="tpu_custom_call" | custom-call | tf_op jit(solution)/shard_map/pallas_call | solution.py:86
  2.8 16.3 %all-gather = f32[128,128]{1,0:T(8,128)S(1)} all-gather(f32[64,128]{1,0:T(8,128)S(1)} %get-tuple-element.11), channel_id=2, replica_groups={{0,1},{2,3},{4,5},{6,7},{8,9},{10,11},{12,13},{14,15},{16,17},{18,19},{..., dimensions={0}, use_global_device_ids=true | all-gather | bytes 98304 | tf_op jit(solution)/shard_map/all_gather | solution.py:266
  19.2 19.3 %all-gather.1 = f32[64,128]{1,0:T(8,128)S(1)} all-gather(f32[32,128]{1,0:T(8,128)S(1)} %slice.31), channel_id=3, replica_groups={{0,3},{1,2},{4,7},{5,6},{8,11},{9,10},{12,15},{13,14},{16,19},{17,18},{..., dimensions={0}, use_global_device_ids=true | all-gather | bytes 49152 | tf_op jit(solution)/shard_map/all_gather | solution.py:266
  38.5 17.0 %all_to_all.15.tiles = f32[8,40,128]{2,1,0:T(8,128)S(1)} all-to-all(f32[8,40,128]{2,1,0:T(8,128)S(1)} %broadcast_in_dim.7), channel_id=1, replica_groups={{0,4,8,12,16,20,24,28},{32,36,40,44,48,52,56,60},{64,68,72,76,80,84,88,..., dimensions={0} | all-to-all | bytes 327680 | tf_op jit(solution)/shard_map/all_to_all | solution.py:276
  55.5 0.9 broadcast_in_dim.8
  56.4 4.0 %all-to-all-start.1 = ((f32[32,40,128]{2,1,0:T(8,128)}), f32[32,40,128]{2,1,0:T(8,128)S(1)}, u32[]{:S(2)}, u32[]{:S(2)}) async-start(f32[32,40,128]{2,1,0:T(8,128)} %bitcast.1), calls=%async_computation.1 | async-start | bytes 1310720 | tf_op jit(solution)/shard_map/all_to_all | solution.py:280
  60.4 0.0 copy-done
  60.4 3.1 %shard_map.74 = (f32[32,128,128]{2,1,0:T(8,128)S(1)}, f32[3,128,128]{2,1,0:T(8,128)S(1)}) custom-call(f32[3,128]{1,0:T(4,128)S(1)} %copy-done, f32[8,40,128]{2,1,0:T(8,128)S(1)} %all_to_all.15.tiles), custom_call_target="tpu_custom_call" | custom-call | flops 1073741824 | bytes 4194304 | tf_op jit(solution)/shard_map/pallas_call | solution.py:239
  63.5 4.5 %all-to-all-done.1.tiles = f32[32,40,128]{2,1,0:T(8,128)S(1)} async-done(((f32[32,40,128]{2,1,0:T(8,128)}), f32[32,40,128]{2,1,0:T(8,128)S(1)}, u32[]{:S(2)}, u32[]{:S(2)}) %all-to-all-start.1) | async-done | bytes 655392 | tf_op jit(solution)/shard_map/all_to_all | solution.py:280
  68.0 7.7 %shard_map.75 = f32[8,32,128]{2,1,0:T(8,128)S(1)} custom-call(f32[32,40,128]{2,1,0:T(8,128)S(1)} %all-to-all-done.1.tiles, f32[32,128,128]{2,1,0:T(8,128)S(1)} %get-tuple-element.13.begun, f32[3,128,128]{2,1,0:T(8,128)S(1)} %get-tuple-element.14.spread), custom_call_target="tpu_custom_call" | custom-call | tf_op jit(solution)/shard_map/pallas_call | solution.py:254
  75.7 16.2 %all_to_all.16 = f32[8,32,128]{2,1,0:T(8,128)S(1)} all-to-all(f32[8,32,128]{2,1,0:T(8,128)S(1)} %shard_map.75), channel_id=1, replica_groups=mesh['sect'=8,'blk'=32,'obs'=4] {'sect'}, dimensions={0} | all-to-all | bytes 262144 | tf_op jit(solution)/shard_map/all_to_all | solution.py:285
  91.9 0.6 reduce_sum.9
  (5 shorter events, 0.0 us)
Async XLA Ops:
  0.0 60.4 %copy-start = (f32[3,128]{1,0:T(4,128)S(1)}, f32[3,128]{1,0:T(4,128)}, u32[]{:S(2)}) copy-start(f32[3,128]{1,0:T(4,128)} %observers.1) | copy-start | bytes 4612
  56.4 11.6 %all-to-all-start.1 = ((f32[32,40,128]{2,1,0:T(8,128)}), f32[32,40,128]{2,1,0:T(8,128)S(1)}, u32[]{:S(2)}, u32[]{:S(2)}) async-start(f32[32,40,128]{2,1,0:T(8,128)} %bitcast.1), calls=%async_computation.1 | async-start | bytes 1310720 | tf_op jit(solution)/shard_map/all_to_all | solution.py:280
